TPU v7x, 512 devices: a whole 4x8x8 slice. The times are simulated.
512 devices in a mesh: resp: 64 (over y, x, z_hi), head: 8 (over z_lo, core).
Axes of the slice: x: 4, y: 8, z: 8 (z_hi: 2, z_lo: 4; z = z_hi * 4 + z_lo), core: 2. Of those that a mesh axis runs over, the one named last changes fastest.
Arguments:
- queries: bfloat16 [16384, 8192], P(('resp', 'head')), may hold values from -6 to 6
- resp_keys: bfloat16 [16384, 1024], P(('resp', 'head')), may hold values from -6 to 6
- resp_values: bfloat16 [16384, 1024], P(('resp', 'head')), may hold values from -6 to 6
- out_grad: bfloat16 [16384, 8192], P(('resp', 'head')), may hold values from -6 to 6
- prompt_keys: bfloat16 [1024, 1024], P(('resp', 'head')), may hold values from -10 to 10
- prompt_values: bfloat16 [1024, 1024], P(('resp', 'head')), may hold values from -6 to 6
- lengths: int32 [64, 4], P('resp'), may hold values from 1 to 160, 256 in all within a row
Outputs:
- attention: bfloat16 [16384, 8192], P(('resp', 'head'))
- query_grad: bfloat16 [16384, 8192], P(('resp', 'head'))
- resp_key_grad: bfloat16 [16384, 1024], P(('resp', 'head'))
- resp_value_grad: bfloat16 [16384, 1024], P(('resp', 'head'))
- prompt_key_grad: float32 [1024, 1024], P(('resp', 'head'))
- prompt_value_grad: float32 [1024, 1024], P(('resp', 'head'))
All inputs are finite; a program needn't handle non-finite values.
Results may differ from a plain program's by a relative error of at most 0.035.
Values may be sent and summed in bfloat16 or wider, within the bound.
No kernel may reach another device: no remote copies, remote signals or barrier semaphores. Data moves between devices by JAX's collectives and lax.ppermute only.
A program may use at most 64 MiB of HBM per device.

v0:
```python
import math

import jax
import jax.numpy as jnp
from jax import lax
from jax.sharding import PartitionSpec as P

DH = 128


def response_mask(seg_lengths, buffer_rows):
    seg_ends = jnp.cumsum(seg_lengths)
    positions = jnp.arange(buffer_rows, dtype=jnp.int32)
    starts = jnp.max(
        jnp.where(seg_ends[None, :] <= positions[:, None], seg_ends[None, :], 0), axis=1
    )
    return (positions[None, :] >= starts[:, None]) & (positions[None, :] <= positions[:, None])


def on_device(queries, resp_keys, resp_values, out_grad, prompt_keys, prompt_values, lengths):
    score_scale = 1.0 / math.sqrt(DH)
    heads_q, keys_own, values_own, grads_own = (
        lax.all_to_all(queries, "head", split_axis=1, concat_axis=0, tiled=True),
        lax.all_to_all(resp_keys, "head", split_axis=1, concat_axis=0, tiled=True),
        lax.all_to_all(resp_values, "head", split_axis=1, concat_axis=0, tiled=True),
        lax.all_to_all(out_grad, "head", split_axis=1, concat_axis=0, tiled=True),
    )
    buffer_rows = heads_q.shape[0]
    local_q = heads_q.shape[1] // DH
    local_kv = keys_own.shape[1] // DH
    group_size = local_q // local_kv
    row_keys, row_values = (
        lax.all_gather(prompt_keys, "resp", axis=0, tiled=True),
        lax.all_gather(prompt_values, "resp", axis=0, tiled=True),
    )
    shared_keys, shared_values = (
        lax.all_to_all(row_keys, "head", split_axis=1, concat_axis=0, tiled=True),
        lax.all_to_all(row_values, "head", split_axis=1, concat_axis=0, tiled=True),
    )
    prompt_count = shared_keys.shape[0]
    key_total = prompt_count + buffer_rows
    key_list = (
        jnp.concatenate([shared_keys, keys_own], axis=0)
        .reshape(key_total, local_kv, DH)
        .transpose(1, 0, 2)
    )
    value_list = (
        jnp.concatenate([shared_values, values_own], axis=0)
        .reshape(key_total, local_kv, DH)
        .transpose(1, 0, 2)
    )
    key_mask = jnp.concatenate(
        [
            jnp.ones((buffer_rows, prompt_count), dtype=jnp.bool_),
            response_mask(lengths[0], buffer_rows),
        ],
        axis=1,
    )
    query_heads = heads_q.reshape(buffer_rows, local_q, DH).transpose(1, 0, 2)
    grad_heads = grads_own.reshape(buffer_rows, local_q, DH).transpose(1, 0, 2)
    contract_last = (((1,), (1,)), ((), ()))
    contract_first = (((0,), (0,)), ((), ()))

    def one_head(totals, sliced):
        head_index, q_one, g_one = sliced
        kv_index = head_index // group_size
        k_one = lax.dynamic_index_in_dim(key_list, kv_index, 0, False)
        v_one = lax.dynamic_index_in_dim(value_list, kv_index, 0, False)
        scores = (
            lax.dot_general(q_one, k_one, contract_last, preferred_element_type=jnp.float32)
            * score_scale
        )
        scores = jnp.where(key_mask, scores, -jnp.inf)
        row_peak = jnp.max(scores, axis=1, keepdims=True)
        exp_terms = jnp.exp(scores - row_peak)
        weights = exp_terms / jnp.sum(exp_terms, axis=1, keepdims=True)
        weights_bf = weights.astype(jnp.bfloat16)
        head_out = jnp.dot(weights_bf, v_one, preferred_element_type=jnp.float32).astype(
            jnp.bfloat16
        )
        out_delta = jnp.sum(
            g_one.astype(jnp.float32) * head_out.astype(jnp.float32), axis=1, keepdims=True
        )
        dweights = lax.dot_general(g_one, v_one, contract_last, preferred_element_type=jnp.float32)
        dscores = (weights * (dweights - out_delta)).astype(jnp.bfloat16)
        query_grad = (
            jnp.dot(dscores, k_one, preferred_element_type=jnp.float32) * score_scale
        ).astype(jnp.bfloat16)
        key_part = (
            lax.dot_general(dscores, q_one, contract_first, preferred_element_type=jnp.float32)
            * score_scale
        )
        value_part = lax.dot_general(
            weights_bf, g_one, contract_first, preferred_element_type=jnp.float32
        )
        total_k, total_v = totals
        total_k = lax.dynamic_update_index_in_dim(
            total_k, lax.dynamic_index_in_dim(total_k, kv_index, 0, False) + key_part, kv_index, 0
        )
        total_v = lax.dynamic_update_index_in_dim(
            total_v, lax.dynamic_index_in_dim(total_v, kv_index, 0, False) + value_part, kv_index, 0
        )
        return ((total_k, total_v), (head_out, query_grad))

    start = (
        jnp.zeros((local_kv, key_total, DH), jnp.float32),
        jnp.zeros((local_kv, key_total, DH), jnp.float32),
    )
    totals, stacked = lax.scan(
        one_head, start, (jnp.arange(local_q, dtype=jnp.int32), query_heads, grad_heads)
    )
    head_out, query_grad = stacked
    head_out = head_out.transpose(1, 0, 2).reshape(buffer_rows, local_q * DH)
    query_grad = query_grad.transpose(1, 0, 2).reshape(buffer_rows, local_q * DH)
    key_grad = totals[0].transpose(1, 0, 2).reshape(key_total, local_kv * DH)
    value_grad = totals[1].transpose(1, 0, 2).reshape(key_total, local_kv * DH)
    prompt_kpart = key_grad[:prompt_count]
    prompt_vpart = value_grad[:prompt_count]
    own_kgrad = key_grad[prompt_count:].astype(jnp.bfloat16)
    own_vgrad = value_grad[prompt_count:].astype(jnp.bfloat16)
    moved_k, moved_v = (
        lax.all_to_all(
            prompt_kpart.astype(jnp.bfloat16), "head", split_axis=0, concat_axis=1, tiled=True
        ).astype(prompt_kpart.dtype),
        lax.all_to_all(
            prompt_vpart.astype(jnp.bfloat16), "head", split_axis=0, concat_axis=1, tiled=True
        ).astype(prompt_vpart.dtype),
    )
    owner_k, owner_v = (
        lax.psum_scatter(moved_k, "resp", scatter_dimension=0, tiled=True),
        lax.psum_scatter(moved_v, "resp", scatter_dimension=0, tiled=True),
    )
    attention, query_back, key_back, value_back = (
        lax.all_to_all(head_out, "head", split_axis=0, concat_axis=1, tiled=True),
        lax.all_to_all(query_grad, "head", split_axis=0, concat_axis=1, tiled=True),
        lax.all_to_all(own_kgrad, "head", split_axis=0, concat_axis=1, tiled=True),
        lax.all_to_all(own_vgrad, "head", split_axis=0, concat_axis=1, tiled=True),
    )
    return (attention, query_back, key_back, value_back, owner_k, owner_v)


def solution(mesh):
    placed = (
        P(("resp", "head"), None),
        P(("resp", "head"), None),
        P(("resp", "head"), None),
        P(("resp", "head"), None),
        P(("resp", "head"), None),
        P(("resp", "head"), None),
        P("resp", None),
    )
    return jax.shard_map(
        on_device,
        mesh=mesh,
        in_specs=placed,
        out_specs=(
            P(("resp", "head"), None),
            P(("resp", "head"), None),
            P(("resp", "head"), None),
            P(("resp", "head"), None),
            P(("resp", "head"), None),
            P(("resp", "head"), None),
        ),
        check_vma=False,
    )
```

profile of v0, /device:TPU:62, one launch (start us, length us, event | category | flops | bytes accessed | tf_op | source)
XLA Modules:
  0.0 1463.7 jit_solution(4196209046698902128)
XLA Ops:
  8.7 7.3 all-to-all-start.2
  15.9 1.5 copy_bitcast_fusion.4
  17.4 4.4 all-to-all-done.2
  21.8 3.4 all-to-all-start.5
  25.2 217.1 %all-gather = bf16[64,2,1024]{2,1,0:T(2,128)(2,1)S(1)} all-gather(bf16[1,2,1024]{2,1,0:T(2,128)(2,1)} %bitcast.175), channel_id=1, replica_groups=mesh['resp'=64,'head'=8] {'resp'}, dimensions={0}, use_global_device_ids=true | all-gather | bytes 266240 | tf_op jit(solution)/shard_map/all_gather | solution.py:33
  243.2 5.2 all-to-all-start.1
  248.3 216.8 %all-gather.1 = bf16[64,2,1024]{2,1,0:T(2,128)(2,1)S(1)} all-gather(bf16[1,2,1024]{2,1,0:T(2,128)(2,1)S(1)} %bitcast.176), channel_id=1, replica_groups=mesh['resp'=64,'head'=8] {'resp'}, dimensions={0}, use_global_device_ids=true | all-gather | bytes 266240 | tf_op jit(solution)/shard_map/all_gather | solution.py:34
  466.0 5.1 all-to-all-start.4
  472.0 8.9 all-to-all-done.4
  480.9 3.5 all-to-all-start
  485.3 14.4 all-to-all-done
  499.7 3.5 all-to-all-start.3
  504.1 14.4 all-to-all-done.3
  519.0 34.8 %while.17 = (s32[]{:T(128)}, f32[1,1280,128]{2,1,0:T(8,128)S(1)}, f32[1,1280,128]{2,1,0:T(8,128)S(1)}, bf16[8,256,128]{1,2,0:T(8,128)(2,1)}, bf16[8,256,128]{2,1...) while((s32[]{:T(128)}, f32[1,1280,128]{2,1,0:T(8,128)S(1)}, ...), condition=%wide.region_6.7_spmd, body=%wide.region_2.6_spmd.sunk | while | flops 509279488 | bytes 13381761 | solution.py:109
  554.6 3.4 all-to-all-start.9
  558.6 5.2 all-to-all-done.9
  563.8 3.4 all-to-all-start.8
  567.8 5.1 all-to-all-done.8
  573.0 3.4 all-to-all-start.10
  577.1 9.0 all-to-all-done.10
  586.1 3.4 all-to-all-start.11
  589.5 1.4 copy.116
  590.8 1.0 all_to_all.170
  591.9 7.3 all-to-all-done.11
  599.1 3.5 all-to-all-start.6
  604.2 1.0 copy.125
  606.6 11.3 all-to-all-done.6
  617.9 3.5 all-to-all-start.7
  621.4 1.3 dynamic-slice
  625.4 13.2 all-to-all-done.7
  639.5 816.0 %all-reduce.6.cloned.1.call-done = (f32[128,1024]{1,0:T(8,128)}, f32[128,1024]{1,0:T(8,128)}) async-done(((f32[128,1024]{1,0:T(8,128)}, f32[128,1024]{1,0:T(8,128)}), (f32[128,1024]{1,0:T(8,128)}, f32[128,1024]{1,0:T(8,128)})) %all-reduce.6.cloned.1.call-update) | async-done | bytes 1048592
  1455.4 1.4 constant_dynamic-slice_fusion
  (119 shorter events, 49.4 us)
Async XLA Ops:
  7.2 0.8 copy-start
  7.2 241.2 %copy-start.4 = (bf16[2,1024]{1,0:T(2,128)(2,1)S(1)}, bf16[2,1024]{1,0:T(2,128)(2,1)}, u32[]{:S(2)}) copy-start(bf16[2,1024]{1,0:T(2,128)(2,1)} %param.14) | copy-start | bytes 12292
  8.7 13.2 all-to-all-start.2
  21.8 221.3 %all-to-all-start.5 = ((bf16[32,8,128]{2,0,1:T(8,128)(2,1)}), bf16[32,8,128]{2,0,1:T(8,128)(2,1)S(1)}, u32[]{:S(2)}, u32[]{:S(2)}) async-start(bf16[32,8,128]{2,0,1:T(8,128)(2,1)} %copy_bitcast_fusion.4), calls=%async_computation.5 | async-start | bytes 131072 | tf_op jit(solution)/shard_map/all_to_all | solution.py:25
  243.2 228.0 %copy-start.1 = (bf16[32,8192]{1,0:T(8,128)(2,1)S(1)}, bf16[32,8192]{1,0:T(8,128)(2,1)}, u32[]{:S(2)}) copy-start(bf16[32,8192]{1,0:T(8,128)(2,1)} %param.9) | copy-start | bytes 1572868
  243.2 222.9 %all-to-all-start.1 = ((bf16[128,8,128]{2,0,1:T(8,128)(2,1)}), bf16[128,8,128]{2,0,1:T(8,128)(2,1)S(1)}, u32[]{:S(2)}, u32[]{:S(2)}) async-start(bf16[128,8,128]{2,0,1:T(8,128)(2,1)} %copy.108), calls=%async_computation.1 | async-start | bytes 524288 | tf_op jit(solution)/shard_map/all_to_all | solution.py:37
  466.0 18.4 %copy-start.2 = (bf16[32,8192]{1,0:T(8,128)(2,1)S(1)}, bf16[32,8192]{1,0:T(8,128)(2,1)}, u32[]{:S(2)}) copy-start(bf16[32,8192]{1,0:T(8,128)(2,1)} %param.12) | copy-start | bytes 1572868
  466.0 14.9 %all-to-all-start.4 = ((bf16[128,8,128]{2,0,1:T(8,128)(2,1)}), bf16[128,8,128]{2,0,1:T(8,128)(2,1)S(1)}, u32[]{:S(2)}, u32[]{:S(2)}) async-start(bf16[128,8,128]{2,0,1:T(8,128)(2,1)} %copy.111), calls=%async_computation.4 | async-start | bytes 524288 | tf_op jit(solution)/shard_map/all_to_all | solution.py:38
  480.9 18.8 %all-to-all-start = ((bf16[32,8,1024]{2,0,1:T(8,128)(2,1)}), bf16[32,8,1024]{2,0,1:T(8,128)(2,1)S(1)}, u32[]{:S(2)}, u32[]{:S(2)}) async-start(bf16[32,8,1024]{2,0,1:T(8,128)(2,1)} %bitcast.123), calls=%async_computation | async-start | bytes 1048576 | tf_op jit(solution)/shard_map/all_to_all | solution.py:23
  484.4 18.8 %copy-start.5 = (s32[1,4]{1,0:T(1,128)S(1)}, s32[1,4]{1,0:T(1,128)}, u32[]{:S(2)}) copy-start(s32[1,4]{1,0:T(1,128)} %param.15) | copy-start | bytes 52
  499.7 18.8 %all-to-all-start.3 = ((bf16[32,8,1024]{2,0,1:T(8,128)(2,1)}), bf16[32,8,1024]{2,0,1:T(8,128)(2,1)S(1)}, u32[]{:S(2)}, u32[]{:S(2)}) async-start(bf16[32,8,1024]{2,0,1:T(8,128)(2,1)} %bitcast.122), calls=%async_computation.3 | async-start | bytes 1048576 | tf_op jit(solution)/shard_map/all_to_all | solution.py:26
  554.6 9.2 all-to-all-start.9
  563.8 9.2 all-to-all-start.8
  573.0 13.1 all-to-all-start.10
  586.1 13.1 all-to-all-start.11
  599.1 18.8 %all-to-all-start.6 = ((bf16[8,32,1024]{2,1,0:T(8,128)(2,1)}), bf16[8,32,1024]{2,1,0:T(8,128)(2,1)S(1)}, u32[]{:S(2)}, u32[]{:S(2)}) async-start(bf16[8,32,1024]{2,1,0:T(8,128)(2,1)} %all_to_all.170), calls=%async_computation.6 | async-start | bytes 1048576 | tf_op jit(solution)/shard_map/all_to_all | solution.py:134
  602.6 852.8 %all-reduce.6.cloned.1.call-start = ((), (), s32[]{:S(2)}) async-start(), calls=%async_computation.12 | async-start | bytes 2097152
  604.1 1.1 copy-start.3
  617.9 20.7 %all-to-all-start.7 = ((bf16[8,32,1024]{2,1,0:T(8,128)(2,1)}), bf16[8,32,1024]{2,1,0:T(8,128)(2,1)S(1)}, u32[]{:S(2)}, u32[]{:S(2)}) async-start(bf16[8,32,1024]{2,1,0:T(8,128)(2,1)} %all_to_all.174), calls=%async_computation.7 | async-start | bytes 1048576 | tf_op jit(solution)/shard_map/all_to_all | solution.py:135
Sparse Core Ops, SparseCore 0:
  606.4 848.9 all-reduce.5
where the time goes:
time: 1470 us; the launch traced here: 1460 us
  waiting for transfers between devices  909 us (62%)
  blocking collectives  434 us (30%)
  starting transfers between devices  48.5 us (3%)
  local copies, waits for them, and re-layouts  26.8 us (2%)
  matrix products  26.8 us (2%)
  between operations  15 us (1%)
    unnamed x2, waiting for transfers between devices  816 us
    all_gather x1, blocking collectives, on_device(): lax.all_gather(prompt_keys, 'resp', axis=0, tiled=True)  217 us
    all_gather x1, blocking collectives, on_device(): lax.all_gather(prompt_values, 'resp', axis=0, tiled=True)  217 us
  transfers between devices with their start and end apart: 13, of which 11 were waited for; matrix products, arithmetic and copies ran while one was open for 1% of the time, Pallas kernels for 0%

commit v1 on v0

v1 whole, which is shorter than its diff:
```python
import functools
import math

import jax
import jax.numpy as jnp
from jax import lax
from jax.experimental import pallas as pl
from jax.experimental.pallas import tpu as pltpu
from jax.sharding import Mesh, PartitionSpec as P

DH = 128
AXES = ("y", "x", "z_hi", "z_lo", "core")
ROW_AXES = ("y", "x")
Z_AXES = ("z_hi", "z_lo", "core")
HEAD_AXES = ("z_lo", "core")
PEERS = 8
SLOTS = 4
ROWS = 32
GROUP = 8
QCOLS = GROUP * DH
BLOCK_COLS = 2 * QCOLS + 2 * DH
OWN = PEERS * ROWS
PLACES = 32
PROMPT = PLACES * 32
KEYS = PROMPT + OWN
CHUNK = 256
SCALE = 1.0 / math.sqrt(DH)
EXP2_SCALE = SCALE * math.log2(math.e)
ANY = pl.BlockSpec(memory_space=pl.ANY)
SMEM = pl.BlockSpec(memory_space=pltpu.SMEM)


def cut_at(peer):
    wide = pl.ds(pl.multiple_of(peer * QCOLS, QCOLS), QCOLS)
    narrow = pl.ds(pl.multiple_of(peer * DH, DH), DH)
    return (
        (wide, pl.ds(0, QCOLS)),
        (wide, pl.ds(QCOLS, QCOLS)),
        (narrow, pl.ds(2 * QCOLS, DH)),
        (narrow, pl.ds(2 * QCOLS + DH, DH)),
    )


def pack_kernel(me_ref, q_ref, g_ref, k_ref, v_ref, *rest):
    outs, sems = rest[:PEERS], rest[PEERS]
    copies = []
    for s in range(PEERS):
        peer = me_ref[0] ^ s
        for n, (src, (here, there)) in enumerate(zip((q_ref, g_ref, k_ref, v_ref), cut_at(peer))):
            copies.append(
                pltpu.make_async_copy(src.at[:, here], outs[s].at[:, there], sems.at[s * 4 + n])
            )
    for copy in copies:
        copy.start()
    for copy in copies:
        copy.wait()


def unpack_kernel(me_ref, *rest):
    blocks, outs, sems = rest[:PEERS], rest[PEERS : PEERS + 4], rest[PEERS + 4]
    copies = []
    for s in range(PEERS):
        peer = me_ref[0] ^ s
        for n, (dst, (here, there)) in enumerate(zip(outs, cut_at(peer))):
            copies.append(
                pltpu.make_async_copy(blocks[s].at[:, there], dst.at[:, here], sems.at[s * 4 + n])
            )
    for copy in copies:
        copy.start()
    for copy in copies:
        copy.wait()


def attend_kernel(me_ref, len_ref, prompt_ref, *rest):
    blocks = rest[:PEERS]
    outs = rest[PEERS : 2 * PEERS]
    (
        prompt_out, held, prompt_held, keys, values, keys_t, values_t,
        dkeys, dvalues, s_ref, p_ref, d_ref, made, prompt_made, sems, out_sems,
    ) = rest[2 * PEERS :]
    me = me_ref[0]
    ins = [pltpu.make_async_copy(prompt_ref, prompt_held, sems.at[PEERS])]
    for s in range(PEERS):
        ins.append(pltpu.make_async_copy(blocks[s], held.at[me ^ s], sems.at[s]))
    for copy in ins:
        copy.start()
    for copy in ins:
        copy.wait()
    for n, (natural, turned) in enumerate(((keys, keys_t), (values, values_t))):
        natural[:PROMPT, :] = prompt_held[:, n].reshape(PROMPT, DH)
        natural[PROMPT:, :] = held[:, :, 2 * QCOLS + n * DH : 2 * QCOLS + (n + 1) * DH].reshape(OWN, DH)
        for c in range(KEYS // CHUNK):
            turned[:, c * CHUNK : (c + 1) * CHUNK] = natural[c * CHUNK : (c + 1) * CHUNK, :].T
    dkeys[...] = jnp.zeros_like(dkeys)
    dvalues[...] = jnp.zeros_like(dvalues)
    ends = []
    total = jnp.int32(0)
    for n in range(SLOTS):
        total = total + len_ref[0, n]
        ends.append(total)
    lanes = lax.broadcasted_iota(jnp.int32, (1, GROUP * ROWS), 1)
    key_at = lax.broadcasted_iota(jnp.int32, (OWN, GROUP * ROWS), 0)
    chunks = [slice(c * CHUNK, (c + 1) * CHUNK) for c in range(KEYS // CHUNK)]

    def one_block(j, carry):
        q = jnp.concatenate([held[j, :, h * DH : (h + 1) * DH] for h in range(GROUP)], axis=0)
        g = jnp.concatenate(
            [held[j, :, QCOLS + h * DH : QCOLS + (h + 1) * DH] for h in range(GROUP)], axis=0
        )
        q_t, g_t = q.T, g.T
        row = j * ROWS + (lanes & (ROWS - 1))
        first = jnp.zeros_like(row)
        for end in ends:
            first = jnp.maximum(first, jnp.where(end <= row, end, 0))
        seen = (key_at >= first) & (key_at <= row)
        peak = jnp.full((8, GROUP * ROWS), -jnp.inf, jnp.float32)
        for c in chunks:
            s = jnp.dot(keys[c, :], q_t, preferred_element_type=jnp.float32)
            if c.start >= PROMPT:
                s = jnp.where(seen, s, -jnp.inf)
            s_ref[c, :] = s
            peak = jnp.maximum(peak, jnp.max(s.reshape(CHUNK // 8, 8, GROUP * ROWS), axis=0))
        peak = jnp.max(peak, axis=0, keepdims=True) * EXP2_SCALE
        norm = jnp.zeros((8, GROUP * ROWS), jnp.float32)
        for c in chunks:
            e = jnp.exp2(s_ref[c, :] * EXP2_SCALE - peak)
            s_ref[c, :] = e
            norm = norm + jnp.sum(e.reshape(CHUNK // 8, 8, GROUP * ROWS), axis=0)
        inverse = 1.0 / jnp.sum(norm, axis=0, keepdims=True)
        for c in chunks:
            w = s_ref[c, :] * inverse
            s_ref[c, :] = w
            w = w.astype(jnp.bfloat16)
            p_ref[c, :] = w
            dvalues[c, :] += jnp.dot(w, g, preferred_element_type=jnp.float32)
        out_t = jnp.dot(values_t[...], p_ref[...], preferred_element_type=jnp.float32)
        out_t = out_t.astype(jnp.bfloat16)
        delta = jnp.sum(
            g_t.astype(jnp.float32) * out_t.astype(jnp.float32), axis=0, keepdims=True
        )
        for c in chunks:
            dw = jnp.dot(values[c, :], g_t, preferred_element_type=jnp.float32)
            ds = (s_ref[c, :] * (dw - delta)).astype(jnp.bfloat16)
            d_ref[c, :] = ds
            dkeys[c, :] += jnp.dot(ds, q, preferred_element_type=jnp.float32)
        dq_t = jnp.dot(keys_t[...], d_ref[...], preferred_element_type=jnp.float32) * SCALE
        out = out_t.T
        dq = dq_t.astype(jnp.bfloat16).T
        for h in range(GROUP):
            made[j, :, h * DH : (h + 1) * DH] = out[h * ROWS : (h + 1) * ROWS, :]
            made[j, :, QCOLS + h * DH : QCOLS + (h + 1) * DH] = dq[h * ROWS : (h + 1) * ROWS, :]
        return carry

    lax.fori_loop(0, PEERS, one_block, 0)
    for n, (grads, factor) in enumerate(((dkeys, SCALE), (dvalues, 1.0))):
        prompt_made[:, n] = (
            (grads[:PROMPT, :] * factor).astype(jnp.bfloat16).reshape(PLACES, PROMPT // PLACES, DH)
        )
        made[:, :, 2 * QCOLS + n * DH : 2 * QCOLS + (n + 1) * DH] = (
            (grads[PROMPT:, :] * factor).astype(jnp.bfloat16).reshape(PEERS, ROWS, DH)
        )
    backs = [pltpu.make_async_copy(prompt_made, prompt_out, out_sems.at[PEERS])]
    for s in range(PEERS):
        backs.append(pltpu.make_async_copy(made.at[me ^ s], outs[s], out_sems.at[s]))
    for copy in backs:
        copy.start()
    for copy in backs:
        copy.wait()


def exchange(blocks):
    moved = [blocks[0]]
    for s in range(1, PEERS):
        moved.append(lax.ppermute(blocks[s], HEAD_AXES, [(i, i ^ s) for i in range(PEERS)]))
    return moved


def on_device(queries, resp_keys, resp_values, out_grad, prompt_keys, prompt_values, lengths):
    bf16 = jnp.bfloat16
    me = lax.axis_index(HEAD_AXES).astype(jnp.int32).reshape(1)
    block = jax.ShapeDtypeStruct((ROWS, BLOCK_COLS), bf16)
    own_rows = prompt_keys.shape[0]

    by_head = jnp.stack(
        [prompt_keys.reshape(own_rows, PEERS, DH), prompt_values.reshape(own_rows, PEERS, DH)]
    ).transpose(2, 0, 1, 3)
    by_head = jnp.broadcast_to(by_head[None], (2,) + by_head.shape).reshape(16, 2, own_rows, DH)
    line = lax.all_to_all(by_head, Z_AXES, split_axis=0, concat_axis=0, tiled=True)
    line = line.transpose(1, 0, 2, 3).reshape(2, 16 * own_rows, DH)
    spread = jnp.broadcast_to(line[None], (PLACES,) + line.shape)
    prompt = lax.all_to_all(spread, ROW_AXES, split_axis=0, concat_axis=0, tiled=True)

    packed = pl.pallas_call(
        pack_kernel,
        out_shape=[block] * PEERS,
        in_specs=[SMEM] + [ANY] * 4,
        out_specs=[ANY] * PEERS,
        scratch_shapes=[pltpu.SemaphoreType.DMA((4 * PEERS,))],
        name="pack",
    )(me, queries, out_grad, resp_keys, resp_values)
    held = exchange(packed)

    width = GROUP * ROWS
    made = pl.pallas_call(
        attend_kernel,
        out_shape=[block] * PEERS + [jax.ShapeDtypeStruct(prompt.shape, bf16)],
        in_specs=[SMEM, SMEM] + [ANY] * (PEERS + 1),
        out_specs=[ANY] * (PEERS + 1),
        scratch_shapes=[
            pltpu.VMEM((PEERS, ROWS, BLOCK_COLS), bf16),
            pltpu.VMEM((PLACES, 2, PROMPT // PLACES, DH), bf16),
            pltpu.VMEM((KEYS, DH), bf16),
            pltpu.VMEM((KEYS, DH), bf16),
            pltpu.VMEM((DH, KEYS), bf16),
            pltpu.VMEM((DH, KEYS), bf16),
            pltpu.VMEM((KEYS, DH), jnp.float32),
            pltpu.VMEM((KEYS, DH), jnp.float32),
            pltpu.VMEM((KEYS, width), jnp.float32),
            pltpu.VMEM((KEYS, width), bf16),
            pltpu.VMEM((KEYS, width), bf16),
            pltpu.VMEM((PEERS, ROWS, BLOCK_COLS), bf16),
            pltpu.VMEM((PLACES, 2, PROMPT // PLACES, DH), bf16),
            pltpu.SemaphoreType.DMA((PEERS + 1,)),
            pltpu.SemaphoreType.DMA((PEERS + 1,)),
        ],
        compiler_params=pltpu.CompilerParams(vmem_limit_bytes=40 * 2**20),
        cost_estimate=pl.CostEstimate(
            flops=12 * PEERS * width * KEYS * DH,
            bytes_accessed=4 * 2**20,
            transcendentals=PEERS * width * KEYS,
        ),
        name="attend",
    )(me, lengths, prompt, *held)
    prompt_part = made[PEERS]

    moved = lax.all_to_all(prompt_part, ROW_AXES, split_axis=0, concat_axis=0, tiled=True)
    summed = jnp.sum(moved.astype(jnp.float32), axis=0)
    summed = summed.reshape(2, 16, own_rows, DH).transpose(1, 0, 2, 3)
    owned = lax.all_to_all(summed, Z_AXES, split_axis=0, concat_axis=0, tiled=True)
    owned = jnp.sum(owned.reshape(2, PEERS, 2, own_rows, DH), axis=0)
    owned = owned.transpose(1, 2, 0, 3).reshape(2, own_rows, PEERS * DH)

    back = exchange(made[:PEERS])
    results = pl.pallas_call(
        unpack_kernel,
        out_shape=[jax.ShapeDtypeStruct(a.shape, bf16) for a in (queries, queries, resp_keys, resp_values)],
        in_specs=[SMEM] + [ANY] * PEERS,
        out_specs=[ANY] * 4,
        scratch_shapes=[pltpu.SemaphoreType.DMA((4 * PEERS,))],
        name="unpack",
    )(me, *back)
    return (*results, owned[0], owned[1])


def solution(mesh):
    fine = Mesh(mesh.devices.reshape(8, 4, 2, 4, 2), AXES)
    rows = P(AXES, None)
    return jax.shard_map(
        on_device,
        mesh=fine,
        in_specs=(rows,) * 6 + (P(("y", "x", "z_hi"), None),),
        out_specs=(rows,) * 6,
        check_vma=False,
    )
```

time: 1470 us -> 212 us (0.14)
  the two profiles are of different devices: /device:TPU:62 before, /device:TPU:1 now
where the time goes in v1:
time: 212 us; the launch traced here: 209 us
  Pallas kernels  93.7 us (44%)
  starting transfers between devices  71.6 us (34%)
  blocking collectives  19 us (9%)
  waiting for transfers between devices  18.1 us (9%)
  local copies, waits for them, and re-layouts  5.21 us (2%)
    ppermute x14, starting transfers between devices, exchange(): lax.ppermute(blocks[s], HEAD_AXES, [(i, i ^ s) for i in range(PEERS)])  48.7 us
    pallas_call x1, Pallas kernels, on_device(): pl.pallas_call(pack_kernel, out_shape=[block] * PEERS, in_specs=[SMEM] +...  37.1 us
    pallas_call x1, Pallas kernels, on_device(): pl.pallas_call(unpack_kernel, out_shape=[jax.ShapeDtypeStruct(a.shape, bf...  37.1 us
    pallas_call x1, Pallas kernels, on_device(): pl.pallas_call(attend_kernel, out_shape=[block] * PEERS + [jax.ShapeDtype...  19.5 us
    all_to_all x1, blocking collectives, on_device(): lax.all_to_all(by_head, Z_AXES, split_axis=0, concat_axis=0, tiled=True)  19 us
    ppermute x14, waiting for transfers between devices, exchange(): lax.ppermute(blocks[s], HEAD_AXES, [(i, i ^ s) for i in range(PEERS)])  18.1 us
    all_to_all x1, starting transfers between devices, on_device(): lax.all_to_all(spread, ROW_AXES, split_axis=0, concat_axis=0, tiled=True)  9.67 us
    all_to_all x1, starting transfers between devices, on_device(): lax.all_to_all(prompt_part, ROW_AXES, split_axis=0, concat_axis=0, tiled=...  9.49 us
  transfers between devices with their start and end apart: 17, of which 4 were waited for; matrix products, arithmetic and copies ran while one was open for 0% of the time, Pallas kernels for 36%

profile of v1, /device:TPU:1, one launch (start us, length us, event | category | flops | bytes accessed | tf_op | source)
XLA Modules:
  0.0 208.7 jit_solution(5062935072203746297)
XLA Ops:
  0.6 0.7 copy_bitcast_fusion
  1.4 19.0 %all_to_all.20 = bf16[16,2,2,128]{3,2,1,0:T(2,128)(2,1)S(1)} all-to-all(bf16[16,2,2,128]{3,2,1,0:T(2,128)(2,1)S(1)} %bitcast.27), channel_id=1, replica_groups=mesh['y'=8,'x'=4,'z_hi'=2,'z_lo'=4,'core'=2] {'z_hi','z_lo','core'}, dimensions={0} | all-to-all | bytes 32768 | tf_op jit(solution)/shard_map/all_to_all | solution.py:188
  20.4 0.9 broadcast_in_dim.15
  21.3 9.7 %all-to-all-start.1 = ((bf16[32,2,32,128]{3,2,1,0:T(8,128)(2,1)}), bf16[32,2,32,128]{3,2,1,0:T(8,128)(2,1)S(1)}, u32[]{:S(2)}, u32[]{:S(2)}) async-start(bf16[32,2,32,128]{3,2,1,0:T(8,128)(2,1)} %broadcast_in_dim.15), calls=%async_computation.1 | async-start | bytes 1048576 | tf_op jit(solution)/shard_map/all_to_all | solution.py:191
  31.0 37.1 %pack.1 = (bf16[32,2304]{1,0:T(8,128)(2,1)}, bf16[32,2304]{1,0:T(8,128)(2,1)}, bf16[32,2304]{1,0:T(8,128)(2,1)}, bf16[32,2304]{1,0:T(8,128)(2,1)}, bf16[32,2304]...) custom-call(s32[1]{0:T(128)} %bitcast.me_ref, ...), custom_call_target="tpu_custom_call" | custom-call | tf_op jit(solution)/shard_map/pack/pallas_call | solution.py:193
  68.1 2.6 %collective-permute-start = (bf16[32,2304]{1,0:T(8,128)(2,1)}, bf16[32,2304]{1,0:T(8,128)(2,1)S(1)}, u32[]{:S(2)}, u32[]{:S(2)}) collective-permute-start(bf16[32,2304]{1,0:T(8,128)(2,1)} %get-tuple-element.28), channel_id=1, source_target_pairs={{0,1},{1,0},{2,3},{3,2},{4,5},{5,4},{6,7},{7,6},{8,9},{9,8},{10,11... | collective-permute-start | bytes 442376 | tf_op jit(solution)/shard_map/ppermute | solution.py:174
  70.7 2.2 %collective-permute-start.1 = (bf16[32,2304]{1,0:T(8,128)(2,1)}, bf16[32,2304]{1,0:T(8,128)(2,1)S(1)}, u32[]{:S(2)}, u32[]{:S(2)}) collective-permute-start(bf16[32,2304]{1,0:T(8,128)(2,1)} %get-tuple-element.29), channel_id=1, source_target_pairs={{0,2},{1,3},{2,0},{3,1},{4,6},{5,7},{6,4},{7,5},{8,10},{9,11},{10,... | collective-permute-start | bytes 442376 | tf_op jit(solution)/shard_map/ppermute | solution.py:174
  72.9 3.3 %collective-permute-start.2 = (bf16[32,2304]{1,0:T(8,128)(2,1)}, bf16[32,2304]{1,0:T(8,128)(2,1)S(1)}, u32[]{:S(2)}, u32[]{:S(2)}) collective-permute-start(bf16[32,2304]{1,0:T(8,128)(2,1)} %get-tuple-element.30), channel_id=1, source_target_pairs={{0,3},{1,2},{2,1},{3,0},{4,7},{5,6},{6,5},{7,4},{8,11},{9,10},{10,... | collective-permute-start | bytes 442376 | tf_op jit(solution)/shard_map/ppermute | solution.py:174
  76.2 2.2 %collective-permute-start.3 = (bf16[32,2304]{1,0:T(8,128)(2,1)}, bf16[32,2304]{1,0:T(8,128)(2,1)S(1)}, u32[]{:S(2)}, u32[]{:S(2)}) collective-permute-start(bf16[32,2304]{1,0:T(8,128)(2,1)} %get-tuple-element.31), channel_id=1, source_target_pairs={{0,4},{1,5},{2,6},{3,7},{4,0},{5,1},{6,2},{7,3},{8,12},{9,13},{10,... | collective-permute-start | bytes 442376 | tf_op jit(solution)/shard_map/ppermute | solution.py:174
  78.4 4.3 %collective-permute-start.4 = (bf16[32,2304]{1,0:T(8,128)(2,1)}, bf16[32,2304]{1,0:T(8,128)(2,1)S(1)}, u32[]{:S(2)}, u32[]{:S(2)}) collective-permute-start(bf16[32,2304]{1,0:T(8,128)(2,1)} %get-tuple-element.32), channel_id=1, source_target_pairs={{0,5},{1,4},{2,7},{3,6},{4,1},{5,0},{6,3},{7,2},{8,13},{9,12},{10,... | collective-permute-start | bytes 442376 | tf_op jit(solution)/shard_map/ppermute | solution.py:174
  82.7 2.2 %collective-permute-start.5 = (bf16[32,2304]{1,0:T(8,128)(2,1)}, bf16[32,2304]{1,0:T(8,128)(2,1)S(1)}, u32[]{:S(2)}, u32[]{:S(2)}) collective-permute-start(bf16[32,2304]{1,0:T(8,128)(2,1)} %get-tuple-element.33), channel_id=1, source_target_pairs={{0,6},{1,7},{2,4},{3,5},{4,2},{5,3},{6,0},{7,1},{8,14},{9,15},{10,... | collective-permute-start | bytes 442376 | tf_op jit(solution)/shard_map/ppermute | solution.py:174
  85.0 5.0 %collective-permute-start.6 = (bf16[32,2304]{1,0:T(8,128)(2,1)}, bf16[32,2304]{1,0:T(8,128)(2,1)S(1)}, u32[]{:S(2)}, u32[]{:S(2)}) collective-permute-start(bf16[32,2304]{1,0:T(8,128)(2,1)} %get-tuple-element.34), channel_id=1, source_target_pairs={{0,7},{1,6},{2,5},{3,4},{4,3},{5,2},{6,1},{7,0},{8,15},{9,14},{10,... | collective-permute-start | bytes 442376 | tf_op jit(solution)/shard_map/ppermute | solution.py:174
  90.1 7.5 %collective-permute-done.3.rest_4_ = bf16[32,2304]{1,0:T(8,128)(2,1)S(1)} collective-permute-done((bf16[32,2304]{1,0:T(8,128)(2,1)}, bf16[32,2304]{1,0:T(8,128)(2,1)S(1)}, u32[]{:S(2)}, u32[]{:S(2)}) %collective-permute-start.3) | collective-permute-done | bytes 147488 | tf_op jit(solution)/shard_map/ppermute | solution.py:174
  97.6 3.2 %collective-permute-done.4.rest_5_ = bf16[32,2304]{1,0:T(8,128)(2,1)S(1)} collective-permute-done((bf16[32,2304]{1,0:T(8,128)(2,1)}, bf16[32,2304]{1,0:T(8,128)(2,1)S(1)}, u32[]{:S(2)}, u32[]{:S(2)}) %collective-permute-start.4) | collective-permute-done | bytes 147488 | tf_op jit(solution)/shard_map/ppermute | solution.py:174
  100.8 0.9 copy-done.1
  101.7 19.5 %attend.1 = (bf16[32,2304]{1,0:T(8,128)(2,1)S(1)}, bf16[32,2304]{1,0:T(8,128)(2,1)S(1)}, bf16[32,2304]{1,0:T(8,128)(2,1)S(1)}, bf16[32,2304]{1,0:T(8,128)(2,1)S(...) custom-call(s32[1]{0:T(128)} %bitcast.me_ref, ...), custom_call_target="tpu_custom_call" | custom-call | flops 4026531840 | bytes 4194304 | tf_op jit(solution)/shard_map/attend/pallas_call | solution.py:204
  121.2 0.7 copy-done
  121.8 9.5 %all-to-all-start.2 = ((bf16[32,2,32,128]{3,2,1,0:T(8,128)(2,1)}), bf16[32,2,32,128]{3,2,1,0:T(8,128)(2,1)S(1)}, u32[]{:S(2)}, u32[]{:S(2)}) async-start(bf16[32,2,32,128]{3,2,1,0:T(8,128)(2,1)} %get-tuple-element.47), calls=%async_computation.2 | async-start | bytes 1048576 | tf_op jit(solution)/shard_map/all_to_all | solution.py:236
  131.3 2.6 %collective-permute-start.7 = (bf16[32,2304]{1,0:T(8,128)(2,1)S(1)}, bf16[32,2304]{1,0:T(8,128)(2,1)S(1)}, u32[]{:S(2)}, u32[]{:S(2)}) collective-permute-start(bf16[32,2304]{1,0:T(8,128)(2,1)S(1)} %get-tuple-element.36), channel_id=1, source_target_pairs={{0,1},{1,0},{2,3},{3,2},{4,5},{5,4},{6,7},{7,6},{8,9},{9,8},{10,11... | collective-permute-start | bytes 442376 | tf_op jit(solution)/shard_map/ppermute | solution.py:174
  133.9 8.5 %collective-permute-start.8 = (bf16[32,2304]{1,0:T(8,128)(2,1)S(1)}, bf16[32,2304]{1,0:T(8,128)(2,1)S(1)}, u32[]{:S(2)}, u32[]{:S(2)}) collective-permute-start(bf16[32,2304]{1,0:T(8,128)(2,1)S(1)} %get-tuple-element.37), channel_id=1, source_target_pairs={{0,2},{1,3},{2,0},{3,1},{4,6},{5,7},{6,4},{7,5},{8,10},{9,11},{10,... | collective-permute-start | bytes 442376 | tf_op jit(solution)/shard_map/ppermute | solution.py:174
  142.4 1.9 collective-permute-start.9
  144.4 2.7 %collective-permute-start.10 = (bf16[32,2304]{1,0:T(8,128)(2,1)S(1)}, bf16[32,2304]{1,0:T(8,128)(2,1)S(1)}, u32[]{:S(2)}, u32[]{:S(2)}) collective-permute-start(bf16[32,2304]{1,0:T(8,128)(2,1)S(1)} %get-tuple-element.39), channel_id=1, source_target_pairs={{0,4},{1,5},{2,6},{3,7},{4,0},{5,1},{6,2},{7,3},{8,12},{9,13},{10,... | collective-permute-start | bytes 442376 | tf_op jit(solution)/shard_map/ppermute | solution.py:174
  147.1 4.0 %collective-permute-start.11 = (bf16[32,2304]{1,0:T(8,128)(2,1)S(1)}, bf16[32,2304]{1,0:T(8,128)(2,1)S(1)}, u32[]{:S(2)}, u32[]{:S(2)}) collective-permute-start(bf16[32,2304]{1,0:T(8,128)(2,1)S(1)} %get-tuple-element.40), channel_id=1, source_target_pairs={{0,5},{1,4},{2,7},{3,6},{4,1},{5,0},{6,3},{7,2},{8,13},{9,12},{10,... | collective-permute-start | bytes 442376 | tf_op jit(solution)/shard_map/ppermute | solution.py:174
  151.1 2.8 %collective-permute-start.12 = (bf16[32,2304]{1,0:T(8,128)(2,1)S(1)}, bf16[32,2304]{1,0:T(8,128)(2,1)S(1)}, u32[]{:S(2)}, u32[]{:S(2)}) collective-permute-start(bf16[32,2304]{1,0:T(8,128)(2,1)S(1)} %get-tuple-element.41), channel_id=1, source_target_pairs={{0,6},{1,7},{2,4},{3,5},{4,2},{5,3},{6,0},{7,1},{8,14},{9,15},{10,... | collective-permute-start | bytes 442376 | tf_op jit(solution)/shard_map/ppermute | solution.py:174
  154.0 4.3 %collective-permute-start.13 = (bf16[32,2304]{1,0:T(8,128)(2,1)S(1)}, bf16[32,2304]{1,0:T(8,128)(2,1)S(1)}, u32[]{:S(2)}, u32[]{:S(2)}) collective-permute-start(bf16[32,2304]{1,0:T(8,128)(2,1)S(1)} %get-tuple-element.42), channel_id=1, source_target_pairs={{0,7},{1,6},{2,5},{3,4},{4,3},{5,2},{6,1},{7,0},{8,15},{9,14},{10,... | collective-permute-start | bytes 442376 | tf_op jit(solution)/shard_map/ppermute | solution.py:174
  158.4 0.6 copy.20
  159.0 3.7 %all-to-all-start.3 = ((f32[16,2,2,128]{3,2,1,0:T(2,128)}), f32[16,2,2,128]{3,2,1,0:T(2,128)S(1)}, u32[]{:S(2)}, u32[]{:S(2)}) async-start(f32[16,2,2,128]{3,2,1,0:T(2,128)} %copy.20), calls=%async_computation.3 | async-start | bytes 65536 | tf_op jit(solution)/shard_map/all_to_all | solution.py:239
  162.7 2.2 %collective-permute-done.10.rest_4_ = bf16[32,2304]{1,0:T(8,128)(2,1)S(1)} collective-permute-done((bf16[32,2304]{1,0:T(8,128)(2,1)S(1)}, bf16[32,2304]{1,0:T(8,128)(2,1)S(1)}, u32[]{:S(2)}, u32[]{:S(2)}) %collective-permute-start.10) | collective-permute-done | bytes 147488 | tf_op jit(solution)/shard_map/ppermute | solution.py:174
  164.9 5.3 %collective-permute-done.11.rest_5_ = bf16[32,2304]{1,0:T(8,128)(2,1)S(1)} collective-permute-done((bf16[32,2304]{1,0:T(8,128)(2,1)S(1)}, bf16[32,2304]{1,0:T(8,128)(2,1)S(1)}, u32[]{:S(2)}, u32[]{:S(2)}) %collective-permute-start.11) | collective-permute-done | bytes 147488 | tf_op jit(solution)/shard_map/ppermute | solution.py:174
  170.2 0.6 copy-done.7
  170.9 37.1 %unpack.1 = (bf16[32,8192]{1,0:T(8,128)(2,1)}, bf16[32,8192]{1,0:T(8,128)(2,1)}, bf16[32,1024]{1,0:T(8,128)(2,1)}, bf16[32,1024]{1,0:T(8,128)(2,1)}) custom-call(s32[1]{0:T(128)} %bitcast.me_ref, bf16[32,2304]{1,0:T(8,128)(2,1)} %copy-done, bf16[32,2304]{1,0:T(8,128)(2,1)} %copy-done.3, bf16[32,2304]{1,0:T(8,128)(2,1)} %copy-done.4, ...), custom_call_target="tpu_custom_call" | custom-call | tf_op jit(solution)/shard_map/unpack/pallas_call | solution.py:244
  208.1 0.6 slice_bitcast_fusion
  (36 shorter events, 0.3 us)
Async XLA Ops:
  21.3 79.5 %all-to-all-start.1 = ((bf16[32,2,32,128]{3,2,1,0:T(8,128)(2,1)}), bf16[32,2,32,128]{3,2,1,0:T(8,128)(2,1)S(1)}, u32[]{:S(2)}, u32[]{:S(2)}) async-start(bf16[32,2,32,128]{3,2,1,0:T(8,128)(2,1)} %broadcast_in_dim.15), calls=%async_computation.1 | async-start | bytes 1048576 | tf_op jit(solution)/shard_map/all_to_all | solution.py:191
  68.1 14.6 %collective-permute-start = (bf16[32,2304]{1,0:T(8,128)(2,1)}, bf16[32,2304]{1,0:T(8,128)(2,1)S(1)}, u32[]{:S(2)}, u32[]{:S(2)}) collective-permute-start(bf16[32,2304]{1,0:T(8,128)(2,1)} %get-tuple-element.28), channel_id=1, source_target_pairs={{0,1},{1,0},{2,3},{3,2},{4,5},{5,4},{6,7},{7,6},{8,9},{9,8},{10,11... | collective-permute-start | bytes 442376 | tf_op jit(solution)/shard_map/ppermute | solution.py:174
  70.7 14.3 %collective-permute-start.1 = (bf16[32,2304]{1,0:T(8,128)(2,1)}, bf16[32,2304]{1,0:T(8,128)(2,1)S(1)}, u32[]{:S(2)}, u32[]{:S(2)}) collective-permute-start(bf16[32,2304]{1,0:T(8,128)(2,1)} %get-tuple-element.29), channel_id=1, source_target_pairs={{0,2},{1,3},{2,0},{3,1},{4,6},{5,7},{6,4},{7,5},{8,10},{9,11},{10,... | collective-permute-start | bytes 442376 | tf_op jit(solution)/shard_map/ppermute | solution.py:174
  72.9 17.2 %collective-permute-start.2 = (bf16[32,2304]{1,0:T(8,128)(2,1)}, bf16[32,2304]{1,0:T(8,128)(2,1)S(1)}, u32[]{:S(2)}, u32[]{:S(2)}) collective-permute-start(bf16[32,2304]{1,0:T(8,128)(2,1)} %get-tuple-element.30), channel_id=1, source_target_pairs={{0,3},{1,2},{2,1},{3,0},{4,7},{5,6},{6,5},{7,4},{8,11},{9,10},{10,... | collective-permute-start | bytes 442376 | tf_op jit(solution)/shard_map/ppermute | solution.py:174
  76.2 21.4 %collective-permute-start.3 = (bf16[32,2304]{1,0:T(8,128)(2,1)}, bf16[32,2304]{1,0:T(8,128)(2,1)S(1)}, u32[]{:S(2)}, u32[]{:S(2)}) collective-permute-start(bf16[32,2304]{1,0:T(8,128)(2,1)} %get-tuple-element.31), channel_id=1, source_target_pairs={{0,4},{1,5},{2,6},{3,7},{4,0},{5,1},{6,2},{7,3},{8,12},{9,13},{10,... | collective-permute-start | bytes 442376 | tf_op jit(solution)/shard_map/ppermute | solution.py:174
  78.4 22.4 %collective-permute-start.4 = (bf16[32,2304]{1,0:T(8,128)(2,1)}, bf16[32,2304]{1,0:T(8,128)(2,1)S(1)}, u32[]{:S(2)}, u32[]{:S(2)}) collective-permute-start(bf16[32,2304]{1,0:T(8,128)(2,1)} %get-tuple-element.32), channel_id=1, source_target_pairs={{0,5},{1,4},{2,7},{3,6},{4,1},{5,0},{6,3},{7,2},{8,13},{9,12},{10,... | collective-permute-start | bytes 442376 | tf_op jit(solution)/shard_map/ppermute | solution.py:174
  82.7 18.0 %collective-permute-start.5 = (bf16[32,2304]{1,0:T(8,128)(2,1)}, bf16[32,2304]{1,0:T(8,128)(2,1)S(1)}, u32[]{:S(2)}, u32[]{:S(2)}) collective-permute-start(bf16[32,2304]{1,0:T(8,128)(2,1)} %get-tuple-element.33), channel_id=1, source_target_pairs={{0,6},{1,7},{2,4},{3,5},{4,2},{5,3},{6,0},{7,1},{8,14},{9,15},{10,... | collective-permute-start | bytes 442376 | tf_op jit(solution)/shard_map/ppermute | solution.py:174
  85.0 15.8 %copy-start.2 = (s32[1,4]{1,0:T(1,128)S(1)}, s32[1,4]{1,0:T(1,128)}, u32[]{:S(2)}) copy-start(s32[1,4]{1,0:T(1,128)} %len_ref.1) | copy-start | bytes 52
  85.0 15.7 %collective-permute-start.6 = (bf16[32,2304]{1,0:T(8,128)(2,1)}, bf16[32,2304]{1,0:T(8,128)(2,1)S(1)}, u32[]{:S(2)}, u32[]{:S(2)}) collective-permute-start(bf16[32,2304]{1,0:T(8,128)(2,1)} %get-tuple-element.34), channel_id=1, source_target_pairs={{0,7},{1,6},{2,5},{3,4},{4,3},{5,2},{6,1},{7,0},{8,15},{9,14},{10,... | collective-permute-start | bytes 442376 | tf_op jit(solution)/shard_map/ppermute | solution.py:174
  100.8 0.9 copy-start.1
  121.2 0.7 copy-start
  121.8 36.4 %all-to-all-start.2 = ((bf16[32,2,32,128]{3,2,1,0:T(8,128)(2,1)}), bf16[32,2,32,128]{3,2,1,0:T(8,128)(2,1)S(1)}, u32[]{:S(2)}, u32[]{:S(2)}) async-start(bf16[32,2,32,128]{3,2,1,0:T(8,128)(2,1)} %get-tuple-element.47), calls=%async_computation.2 | async-start | bytes 1048576 | tf_op jit(solution)/shard_map/all_to_all | solution.py:236
  131.3 19.8 %collective-permute-start.7 = (bf16[32,2304]{1,0:T(8,128)(2,1)S(1)}, bf16[32,2304]{1,0:T(8,128)(2,1)S(1)}, u32[]{:S(2)}, u32[]{:S(2)}) collective-permute-start(bf16[32,2304]{1,0:T(8,128)(2,1)S(1)} %get-tuple-element.36), channel_id=1, source_target_pairs={{0,1},{1,0},{2,3},{3,2},{4,5},{5,4},{6,7},{7,6},{8,9},{9,8},{10,11... | collective-permute-start | bytes 442376 | tf_op jit(solution)/shard_map/ppermute | solution.py:174
  133.9 20.0 %collective-permute-start.8 = (bf16[32,2304]{1,0:T(8,128)(2,1)S(1)}, bf16[32,2304]{1,0:T(8,128)(2,1)S(1)}, u32[]{:S(2)}, u32[]{:S(2)}) collective-permute-start(bf16[32,2304]{1,0:T(8,128)(2,1)S(1)} %get-tuple-element.37), channel_id=1, source_target_pairs={{0,2},{1,3},{2,0},{3,1},{4,6},{5,7},{6,4},{7,5},{8,10},{9,11},{10,... | collective-permute-start | bytes 442376 | tf_op jit(solution)/shard_map/ppermute | solution.py:174
  142.4 20.3 %collective-permute-start.9 = (bf16[32,2304]{1,0:T(8,128)(2,1)S(1)}, bf16[32,2304]{1,0:T(8,128)(2,1)S(1)}, u32[]{:S(2)}, u32[]{:S(2)}) collective-permute-start(bf16[32,2304]{1,0:T(8,128)(2,1)S(1)} %get-tuple-element.38), channel_id=1, source_target_pairs={{0,3},{1,2},{2,1},{3,0},{4,7},{5,6},{6,5},{7,4},{8,11},{9,10},{10,... | collective-permute-start | bytes 442376 | tf_op jit(solution)/shard_map/ppermute | solution.py:174
  144.4 20.5 %collective-permute-start.10 = (bf16[32,2304]{1,0:T(8,128)(2,1)S(1)}, bf16[32,2304]{1,0:T(8,128)(2,1)S(1)}, u32[]{:S(2)}, u32[]{:S(2)}) collective-permute-start(bf16[32,2304]{1,0:T(8,128)(2,1)S(1)} %get-tuple-element.39), channel_id=1, source_target_pairs={{0,4},{1,5},{2,6},{3,7},{4,0},{5,1},{6,2},{7,3},{8,12},{9,13},{10,... | collective-permute-start | bytes 442376 | tf_op jit(solution)/shard_map/ppermute | solution.py:174
  147.1 23.1 %collective-permute-start.11 = (bf16[32,2304]{1,0:T(8,128)(2,1)S(1)}, bf16[32,2304]{1,0:T(8,128)(2,1)S(1)}, u32[]{:S(2)}, u32[]{:S(2)}) collective-permute-start(bf16[32,2304]{1,0:T(8,128)(2,1)S(1)} %get-tuple-element.40), channel_id=1, source_target_pairs={{0,5},{1,4},{2,7},{3,6},{4,1},{5,0},{6,3},{7,2},{8,13},{9,12},{10,... | collective-permute-start | bytes 442376 | tf_op jit(solution)/shard_map/ppermute | solution.py:174
  151.1 7.2 %copy-start.3 = (bf16[32,2304]{1,0:T(8,128)(2,1)}, bf16[32,2304]{1,0:T(8,128)(2,1)S(1)}, u32[]{:S(2)}) copy-start(bf16[32,2304]{1,0:T(8,128)(2,1)S(1)} %collective-permute-done.7.rest_1_) | copy-start | bytes 442372
  151.1 19.0 %collective-permute-start.12 = (bf16[32,2304]{1,0:T(8,128)(2,1)S(1)}, bf16[32,2304]{1,0:T(8,128)(2,1)S(1)}, u32[]{:S(2)}, u32[]{:S(2)}) collective-permute-start(bf16[32,2304]{1,0:T(8,128)(2,1)S(1)} %get-tuple-element.41), channel_id=1, source_target_pairs={{0,6},{1,7},{2,4},{3,5},{4,2},{5,3},{6,0},{7,1},{8,14},{9,15},{10,... | collective-permute-start | bytes 442376 | tf_op jit(solution)/shard_map/ppermute | solution.py:174
  154.0 4.4 %copy-start.4 = (bf16[32,2304]{1,0:T(8,128)(2,1)}, bf16[32,2304]{1,0:T(8,128)(2,1)S(1)}, u32[]{:S(2)}) copy-start(bf16[32,2304]{1,0:T(8,128)(2,1)S(1)} %collective-permute-done.8.rest_2_) | copy-start | bytes 442372
  154.0 16.2 %collective-permute-start.13 = (bf16[32,2304]{1,0:T(8,128)(2,1)S(1)}, bf16[32,2304]{1,0:T(8,128)(2,1)S(1)}, u32[]{:S(2)}, u32[]{:S(2)}) collective-permute-start(bf16[32,2304]{1,0:T(8,128)(2,1)S(1)} %get-tuple-element.42), channel_id=1, source_target_pairs={{0,7},{1,6},{2,5},{3,4},{4,3},{5,2},{6,1},{7,0},{8,15},{9,14},{10,... | collective-permute-start | bytes 442376 | tf_op jit(solution)/shard_map/ppermute | solution.py:174
  159.0 49.1 %all-to-all-start.3 = ((f32[16,2,2,128]{3,2,1,0:T(2,128)}), f32[16,2,2,128]{3,2,1,0:T(2,128)S(1)}, u32[]{:S(2)}, u32[]{:S(2)}) async-start(f32[16,2,2,128]{3,2,1,0:T(2,128)} %copy.20), calls=%async_computation.3 | async-start | bytes 65536 | tf_op jit(solution)/shard_map/all_to_all | solution.py:239
  162.7 7.5 %copy-start.5 = (bf16[32,2304]{1,0:T(8,128)(2,1)}, bf16[32,2304]{1,0:T(8,128)(2,1)S(1)}, u32[]{:S(2)}) copy-start(bf16[32,2304]{1,0:T(8,128)(2,1)S(1)} %collective-permute-done.9.rest_3_) | copy-start | bytes 442372
  164.9 5.3 %copy-start.6 = (bf16[32,2304]{1,0:T(8,128)(2,1)}, bf16[32,2304]{1,0:T(8,128)(2,1)S(1)}, u32[]{:S(2)}) copy-start(bf16[32,2304]{1,0:T(8,128)(2,1)S(1)} %collective-permute-done.10.rest_4_) | copy-start | bytes 442372
  170.1 0.7 copy-start.7
  170.1 0.7 copy-start.8
  170.1 0.8 copy-start.9

commit v2 on v1

v2 whole, which is shorter than its diff:
```python
import functools
import math

import jax
import jax.numpy as jnp
from jax import lax
from jax.experimental import pallas as pl
from jax.experimental.pallas import tpu as pltpu
from jax.sharding import Mesh, PartitionSpec as P

DH = 128
AXES = ("y_hi", "y_lo", "x", "z_hi", "z_lo", "core")
FIRST_AXES = ("y_hi", "z_hi", "z_lo", "core")
HEAD_AXES = ("z_lo", "core")
PEERS = 8
SLOTS = 4
ROWS = 32
GROUP = 8
QCOLS = GROUP * DH
BLOCK_COLS = 2 * QCOLS + 2 * DH
OWN = PEERS * ROWS
FIRST = 32
XS = 4
XROWS = 256
PROMPT = XS * XROWS
KEYS = PROMPT + OWN
CHUNK = 256
STEP = 128
PAIR = 2
WIDTH = PAIR * GROUP * ROWS
FLOOR = -1e30
SCALE = 1.0 / math.sqrt(DH)
EXP2_SCALE = SCALE * math.log2(math.e)
ANY = pl.BlockSpec(memory_space=pl.ANY)
VMEM = pl.BlockSpec(memory_space=pltpu.VMEM)
SMEM = pl.BlockSpec(memory_space=pltpu.SMEM)


def cut_at(peer):
    wide, narrow = pl.ds(peer * QCOLS, QCOLS), pl.ds(peer * DH, DH)
    return (
        (wide, pl.ds(0, QCOLS)),
        (wide, pl.ds(QCOLS, QCOLS)),
        (narrow, pl.ds(2 * QCOLS, DH)),
        (narrow, pl.ds(2 * QCOLS + DH, DH)),
    )


def pack_kernel(q_ref, g_ref, k_ref, v_ref, out, sems):
    copies = []
    for peer in range(PEERS):
        for n, (src, (here, there)) in enumerate(zip((q_ref, g_ref, k_ref, v_ref), cut_at(peer))):
            copies.append(
                pltpu.make_async_copy(src.at[:, here], out.at[peer, :, there], sems.at[peer * 4 + n])
            )
    for copy in copies:
        copy.start()
    for copy in copies:
        copy.wait()


def unpack_kernel(blocks, *rest):
    outs, sems = rest[:4], rest[4]
    copies = []
    for peer in range(PEERS):
        for n, (dst, (here, there)) in enumerate(zip(outs, cut_at(peer))):
            copies.append(
                pltpu.make_async_copy(
                    blocks.at[peer, :, there], dst.at[:, here], sems.at[peer * 4 + n]
                )
            )
    for copy in copies:
        copy.start()
    for copy in copies:
        copy.wait()


def attend_kernel(len_ref, blocks, *rest):
    prompts, outs, prompt_outs, rest = rest[:XS], rest[XS], rest[XS + 1 : 2 * XS + 1], rest[2 * XS + 1 :]
    (
        held, held_kv, prompt_held, keys, values, keys_t, values_t,
        dkeys, dvalues, e_ref, p_ref, d_ref, made, made_kv, prompt_made, sems, out_sems,
    ) = rest
    heads, tail = pl.ds(0, 2 * QCOLS), pl.ds(2 * QCOLS, 2 * DH)
    first_in = [pltpu.make_async_copy(blocks.at[:, :, tail], held_kv, sems.at[PEERS])]
    for a in range(XS):
        first_in.append(pltpu.make_async_copy(prompts[a], prompt_held.at[a], sems.at[PEERS + 1 + a]))
    ins = [
        pltpu.make_async_copy(blocks.at[j, :, heads], held.at[j], sems.at[j]) for j in range(PEERS)
    ]
    for copy in first_in + ins:
        copy.start()
    for copy in first_in:
        copy.wait()
    for n, (natural, turned) in enumerate(((keys, keys_t), (values, values_t))):
        natural[:PROMPT, :] = prompt_held[:, :, n * DH : (n + 1) * DH].reshape(PROMPT, DH)
        natural[PROMPT:, :] = held_kv[:, :, n * DH : (n + 1) * DH].reshape(OWN, DH)
        for c in range(KEYS // CHUNK):
            turned[:, c * CHUNK : (c + 1) * CHUNK] = natural[c * CHUNK : (c + 1) * CHUNK, :].T
    ends = []
    total = jnp.int32(0)
    for n in range(SLOTS):
        total = total + len_ref[0, n]
        ends.append(total)
    lanes = lax.broadcasted_iota(jnp.int32, (1, WIDTH), 1)
    key_at = lax.broadcasted_iota(jnp.int32, (STEP, WIDTH), 0)
    chunks = [slice(c * CHUNK, (c + 1) * CHUNK) for c in range(KEYS // CHUNK)]
    steps = [slice(c * STEP, (c + 1) * STEP) for c in range(KEYS // STEP)]

    def stacked(s, base):
        return jnp.concatenate(
            [
                held[s + n, :, base + h * DH : base + (h + 1) * DH]
                for n in range(PAIR)
                for h in range(GROUP)
            ],
            axis=0,
        )

    outs_going = []
    for s in range(0, PEERS, PAIR):
        for n in range(PAIR):
            ins[s + n].wait()
        q, g = stacked(s, 0), stacked(s, QCOLS)
        q_t, g_t = q.T, g.T
        row = (s + lanes // (GROUP * ROWS)) * ROWS + lanes % ROWS
        start = jnp.zeros_like(row)
        for end in ends:
            start = jnp.maximum(start, jnp.where(end <= row, end, 0))
        peaks, sums = [], []
        for c in steps:
            x = jnp.dot(keys[c, :], q_t, preferred_element_type=jnp.float32)
            if c.start >= PROMPT:
                at = key_at + (c.start - PROMPT)
                x = jnp.where((at >= start) & (at <= row), x, -jnp.inf)
            peak = jnp.maximum(jnp.max(x, axis=0, keepdims=True), FLOOR) * EXP2_SCALE
            e = jnp.exp2(x * EXP2_SCALE - peak)
            e_ref[c, :] = e
            peaks.append(peak)
            sums.append(jnp.sum(e, axis=0, keepdims=True))
        top = functools.reduce(jnp.maximum, peaks)
        factors = [jnp.exp2(peak - top) for peak in peaks]
        inverse = 1.0 / sum(a * b for a, b in zip(factors, sums))
        factors = [factor * inverse for factor in factors]
        for c, factor in zip(steps, factors):
            p_ref[c, :] = (e_ref[c, :] * factor).astype(jnp.bfloat16)
        for c in chunks:
            part = jnp.dot(p_ref[c, :], g, preferred_element_type=jnp.float32)
            if s == 0:
                dvalues[c, :] = part
            else:
                dvalues[c, :] += part
        out_t = jnp.dot(values_t[...], p_ref[...], preferred_element_type=jnp.float32)
        out_t = out_t.astype(jnp.bfloat16)
        delta = jnp.sum(
            g_t.astype(jnp.float32) * out_t.astype(jnp.float32), axis=0, keepdims=True
        )
        for c, factor in zip(steps, factors):
            dw = jnp.dot(values[c, :], g_t, preferred_element_type=jnp.float32)
            d_ref[c, :] = ((e_ref[c, :] * factor) * (dw - delta)).astype(jnp.bfloat16)
        for c in chunks:
            part = jnp.dot(d_ref[c, :], q, preferred_element_type=jnp.float32)
            if s == 0:
                dkeys[c, :] = part
            else:
                dkeys[c, :] += part
        dq_t = jnp.dot(keys_t[...], d_ref[...], preferred_element_type=jnp.float32) * SCALE
        out = out_t.T
        dq = dq_t.astype(jnp.bfloat16).T
        for n in range(PAIR):
            for h in range(GROUP):
                at = slice((n * GROUP + h) * ROWS, (n * GROUP + h + 1) * ROWS)
                made[s + n, :, h * DH : (h + 1) * DH] = out[at, :]
                made[s + n, :, QCOLS + h * DH : QCOLS + (h + 1) * DH] = dq[at, :]
            copy = pltpu.make_async_copy(
                made.at[s + n], outs.at[s + n, :, heads], out_sems.at[s + n]
            )
            copy.start()
            outs_going.append(copy)
    for n, (grads, factor) in enumerate(((dkeys, SCALE), (dvalues, 1.0))):
        prompt_made[:, :, n * DH : (n + 1) * DH] = (
            (grads[:PROMPT, :] * factor).astype(jnp.bfloat16).reshape(XS, XROWS, DH)
        )
        made_kv[:, :, n * DH : (n + 1) * DH] = (
            (grads[PROMPT:, :] * factor).astype(jnp.bfloat16).reshape(PEERS, ROWS, DH)
        )
    backs = [pltpu.make_async_copy(made_kv, outs.at[:, :, tail], out_sems.at[PEERS])]
    for a in range(XS):
        backs.append(
            pltpu.make_async_copy(prompt_made.at[a], prompt_outs[a], out_sems.at[PEERS + 1 + a])
        )
    for copy in backs:
        copy.start()
    for copy in outs_going + backs:
        copy.wait()


def across(value, axis, s):
    n = lax.axis_size(axis)
    return lax.ppermute(value, axis, [(i, i ^ s) for i in range(n)])


def attend(lengths, held, prompt):
    bf16 = jnp.bfloat16
    block = jax.ShapeDtypeStruct((PEERS, ROWS, BLOCK_COLS), bf16)
    piece = jax.ShapeDtypeStruct((XROWS, 2 * DH), bf16)
    return pl.pallas_call(
        attend_kernel,
        out_shape=[block] + [piece] * XS,
        in_specs=[SMEM] + [ANY] * (XS + 1),
        out_specs=[ANY] * (XS + 1),
        scratch_shapes=[
            pltpu.VMEM((PEERS, ROWS, 2 * QCOLS), bf16),
            pltpu.VMEM((PEERS, ROWS, 2 * DH), bf16),
            pltpu.VMEM((XS, XROWS, 2 * DH), bf16),
            pltpu.VMEM((KEYS, DH), bf16),
            pltpu.VMEM((KEYS, DH), bf16),
            pltpu.VMEM((DH, KEYS), bf16),
            pltpu.VMEM((DH, KEYS), bf16),
            pltpu.VMEM((KEYS, DH), jnp.float32),
            pltpu.VMEM((KEYS, DH), jnp.float32),
            pltpu.VMEM((KEYS, WIDTH), jnp.float32),
            pltpu.VMEM((KEYS, WIDTH), bf16),
            pltpu.VMEM((KEYS, WIDTH), bf16),
            pltpu.VMEM((PEERS, ROWS, 2 * QCOLS), bf16),
            pltpu.VMEM((PEERS, ROWS, 2 * DH), bf16),
            pltpu.VMEM((XS, XROWS, 2 * DH), bf16),
            pltpu.SemaphoreType.DMA((PEERS + 1 + XS,)),
            pltpu.SemaphoreType.DMA((PEERS + 1 + XS,)),
        ],
        compiler_params=pltpu.CompilerParams(vmem_limit_bytes=40 * 2**20),
        cost_estimate=pl.CostEstimate(
            flops=12 * PEERS * GROUP * ROWS * KEYS * DH,
            bytes_accessed=4 * 2**20,
            transcendentals=PEERS * GROUP * ROWS * KEYS,
        ),
        name="attend",
    )(lengths, held, *prompt)


def on_device(queries, resp_keys, resp_values, out_grad, prompt_keys, prompt_values, lengths):
    bf16, f32 = jnp.bfloat16, jnp.float32
    own_rows = prompt_keys.shape[0]

    by_head = jnp.concatenate(
        [prompt_keys.reshape(own_rows, PEERS, DH), prompt_values.reshape(own_rows, PEERS, DH)], axis=2
    ).transpose(1, 0, 2)
    by_head = jnp.broadcast_to(by_head[None], (4,) + by_head.shape).reshape(FIRST, own_rows, 2 * DH)
    line = lax.all_to_all(by_head, FIRST_AXES, split_axis=0, concat_axis=0, tiled=True)

    packed = pl.pallas_call(
        pack_kernel,
        out_shape=jax.ShapeDtypeStruct((PEERS, ROWS, BLOCK_COLS), bf16),
        in_specs=[ANY] * 4,
        out_specs=VMEM,
        scratch_shapes=[pltpu.SemaphoreType.DMA((4 * PEERS,))],
        name="pack",
    )(queries, out_grad, resp_keys, resp_values)
    line, packed = lax.optimization_barrier((line, packed))
    held = lax.all_to_all(packed, HEAD_AXES, split_axis=0, concat_axis=0, tiled=True)

    line = line.reshape(FIRST * own_rows, 2 * DH)
    line = jnp.concatenate([line] + [across(line, "y_lo", b) for b in (1, 2, 3)], axis=0)
    prompt = [line] + [across(line, "x", a) for a in (1, 2, 3)]

    made, *parts = attend(lengths, held, prompt)

    back = lax.all_to_all(made, HEAD_AXES, split_axis=0, concat_axis=0, tiled=True)

    total = parts[0].astype(f32)
    for a in (1, 2, 3):
        total = total + across(parts[a], "x", a).astype(f32)
    total = total.astype(bf16).reshape(4, XROWS // 4, 2 * DH)
    pieces = [total[b] for b in range(4)]
    total = pieces[0].astype(f32)
    for b in (1, 2, 3):
        total = total + across(pieces[b], "y_lo", b).astype(f32)
    total, back = lax.optimization_barrier((total, back))
    owned = lax.all_to_all(
        total.reshape(FIRST, own_rows, 2 * DH), FIRST_AXES, split_axis=0, concat_axis=0, tiled=True
    )
    owned = jnp.sum(owned.reshape(4, PEERS, own_rows, 2, DH), axis=0)
    owned = owned.transpose(2, 1, 0, 3).reshape(2, own_rows, PEERS * DH)

    results = pl.pallas_call(
        unpack_kernel,
        out_shape=[jax.ShapeDtypeStruct(a.shape, bf16) for a in (queries, queries, resp_keys, resp_values)],
        in_specs=[ANY],
        out_specs=[VMEM] * 4,
        scratch_shapes=[pltpu.SemaphoreType.DMA((4 * PEERS,))],
        name="unpack",
    )(back)
    return (*results, owned[0], owned[1])


def solution(mesh):
    fine = Mesh(mesh.devices.reshape(2, 4, 4, 2, 4, 2), AXES)
    rows = P(AXES, None)
    return jax.shard_map(
        on_device,
        mesh=fine,
        in_specs=(rows,) * 6 + (P(("y_hi", "y_lo", "x", "z_hi"), None),),
        out_specs=(rows,) * 6,
        check_vma=False,
    )
```

time: 212 us -> 130 us (0.61); the launches traced: 209 us -> 129 us
  Pallas kernels: 93.7 us -> 18.4 us
  waiting for transfers between devices: 18.1 us -> 38.9 us
  blocking collectives: 19 us -> 0 us
  starting transfers between devices: 71.6 us -> 67.9 us
  local copies, waits for them, and re-layouts: 5.21 us -> 2.83 us
    pallas_call x2, Pallas kernels: 56.6 us -> 15.8 us  [the longest x1 13.1 us: attend(): pl.pallas_call(attend_kernel, out_shape=[block] + [piece] * XS, in_specs=...]
    pallas_call x1, Pallas kernels: 37.1 us -> 2.64 us  [on_device(): pl.pallas_call(unpack_kernel, out_shape=[jax.ShapeDtypeStruct(a.shape, bf...]
    all_to_all x3 -> x4, waiting for transfers between devices: 0.01 us -> 24.6 us  [the longest x1 9.19 us: on_device(): lax.all_to_all(total.reshape(FIRST, own_rows, 2 * DH), FIRST_AXES, split_...]
    all_to_all x1 -> x0, blocking collectives: 19 us -> none  [on_device(): lax.all_to_all(by_head, Z_AXES, split_axis=0, concat_axis=0, tiled=True)]
    ppermute x14 -> x12, starting transfers between devices: 48.7 us -> 36.2 us  [across(): return lax.ppermute(value, axis, [(i, i ^ s) for i in range(n)])]
    all_to_all x3 -> x4, starting transfers between devices: 22.9 us -> 31.6 us  [the longest x1 17.2 us: on_device(): lax.all_to_all(by_head, FIRST_AXES, split_axis=0, concat_axis=0, tiled=True)]
    ppermute x14 -> x12, waiting for transfers between devices: 18.1 us -> 14.3 us  [across(): return lax.ppermute(value, axis, [(i, i ^ s) for i in range(n)])]
    unnamed x20 -> x7, local copies, waits for them, and re-layouts: 2.33 us -> 0.02 us
  transfers between devices with their start and end apart: 17 -> 16, of which waited for: 4 -> 11; matrix products, arithmetic and copies ran while one was open for 0% -> 0% of each run, Pallas kernels for 36% -> 4%
where the time goes in v2:
time: 130 us; the launch traced here: 129 us
  starting transfers between devices  67.9 us (52%)
  waiting for transfers between devices  38.9 us (30%)
  Pallas kernels  18.4 us (14%)
  local copies, waits for them, and re-layouts  2.83 us (2%)
    ppermute x12, starting transfers between devices, across(): return lax.ppermute(value, axis, [(i, i ^ s) for i in range(n)])  36.2 us
    all_to_all x1, starting transfers between devices, on_device(): lax.all_to_all(by_head, FIRST_AXES, split_axis=0, concat_axis=0, tiled=True)  17.2 us
    ppermute x12, waiting for transfers between devices, across(): return lax.ppermute(value, axis, [(i, i ^ s) for i in range(n)])  14.3 us
    pallas_call x1, Pallas kernels, attend(): pl.pallas_call(attend_kernel, out_shape=[block] + [piece] * XS, in_specs=...  13.1 us
    all_to_all x1, waiting for transfers between devices, on_device(): lax.all_to_all(total.reshape(FIRST, own_rows, 2 * DH), FIRST_AXES, split_...  9.19 us
    all_to_all x1, waiting for transfers between devices, on_device(): lax.all_to_all(by_head, FIRST_AXES, split_axis=0, concat_axis=0, tiled=True)  9.09 us
    all_to_all x1, starting transfers between devices, on_device(): lax.all_to_all(total.reshape(FIRST, own_rows, 2 * DH), FIRST_AXES, split_...  5.8 us
    all_to_all x1, waiting for transfers between devices, on_device(): lax.all_to_all(packed, HEAD_AXES, split_axis=0, concat_axis=0, tiled=True)  4.52 us
  transfers between devices with their start and end apart: 16, of which 11 were waited for; matrix products, arithmetic and copies ran while one was open for 0% of the time, Pallas kernels for 4%

profile of v2, /device:TPU:1, one launch (start us, length us, event | category | flops | bytes accessed | tf_op | source)
XLA Modules:
  0.0 129.0 jit_solution(11346856917318589621)
XLA Ops:
  0.6 0.7 copy_bitcast_fusion
  1.4 0.6 broadcast_in_dim.2
  2.0 17.2 %all-to-all-start = ((bf16[32,2,256]{2,1,0:T(2,128)(2,1)}), bf16[32,2,256]{2,1,0:T(2,128)(2,1)S(1)}, u32[]{:S(2)}, u32[]{:S(2)}) async-start(bf16[32,2,256]{2,1,0:T(2,128)(2,1)} %bitcast.1), calls=%async_computation | async-start | bytes 65536 | tf_op jit(solution)/shard_map/all_to_all | solution.py:249
  19.2 2.7 %pack.1 = bf16[8,32,2304]{2,1,0:T(8,128)(2,1)} custom-call(bf16[32,8192]{1,0:T(8,128)(2,1)} %q_ref.1, bf16[32,8192]{1,0:T(8,128)(2,1)} %g_ref.1, bf16[32,1024]{1,0:T(8,128)(2,1)} %k_ref.1, bf16[32,1024]{1,0:T(8,128)(2,1)} %v_ref.1), custom_call_target="tpu_custom_call" | custom-call | tf_op jit(solution)/shard_map/pack/pallas_call | solution.py:251
  21.9 9.1 %all-to-all-done = bf16[32,2,256]{2,1,0:T(2,128)(2,1)S(1)} async-done(((bf16[32,2,256]{2,1,0:T(2,128)(2,1)}), bf16[32,2,256]{2,1,0:T(2,128)(2,1)S(1)}, u32[]{:S(2)}, u32[]{:S(2)}) %all-to-all-start) | async-done | bytes 32800 | tf_op jit(solution)/shard_map/all_to_all | solution.py:249
  31.0 4.3 %all-to-all-start.1 = ((bf16[8,32,2304]{2,1,0:T(8,128)(2,1)}), bf16[8,32,2304]{2,1,0:T(8,128)(2,1)S(1)}, u32[]{:S(2)}, u32[]{:S(2)}) async-start(bf16[8,32,2304]{2,1,0:T(8,128)(2,1)} %pack.1), calls=%async_computation.1 | async-start | bytes 2359296 | tf_op jit(solution)/shard_map/all_to_all | solution.py:260
  35.3 2.6 %collective-permute-start.2 = (bf16[64,256]{1,0:T(8,128)(2,1)S(1)}, bf16[64,256]{1,0:T(8,128)(2,1)S(1)}, u32[]{:S(2)}, u32[]{:S(2)}) collective-permute-start(bf16[64,256]{1,0:T(8,128)(2,1)S(1)} %reshape.48), channel_id=1, source_target_pairs={{0,192},{64,128},{128,64},{192,0},{1,193},{65,129},{129,65},{193,1... | collective-permute-start | bytes 98312 | tf_op jit(solution)/shard_map/ppermute | solution.py:200
  37.9 2.9 %collective-permute-start.1 = (bf16[64,256]{1,0:T(8,128)(2,1)S(1)}, bf16[64,256]{1,0:T(8,128)(2,1)S(1)}, u32[]{:S(2)}, u32[]{:S(2)}) collective-permute-start(bf16[64,256]{1,0:T(8,128)(2,1)S(1)} %reshape.48), channel_id=1, source_target_pairs={{0,128},{64,192},{128,0},{192,64},{1,129},{65,193},{129,1},{193,65... | collective-permute-start | bytes 98312 | tf_op jit(solution)/shard_map/ppermute | solution.py:200
  40.7 3.9 %collective-permute-start = (bf16[64,256]{1,0:T(8,128)(2,1)S(1)}, bf16[64,256]{1,0:T(8,128)(2,1)S(1)}, u32[]{:S(2)}, u32[]{:S(2)}) collective-permute-start(bf16[64,256]{1,0:T(8,128)(2,1)S(1)} %reshape.48), channel_id=1, source_target_pairs={{0,64},{64,0},{128,192},{192,128},{1,65},{65,1},{129,193},{193,129... | collective-permute-start | bytes 98312 | tf_op jit(solution)/shard_map/ppermute | solution.py:200
  44.6 1.6 %collective-permute-done = bf16[64,256]{1,0:T(8,128)(2,1)S(1)} collective-permute-done((bf16[64,256]{1,0:T(8,128)(2,1)S(1)}, bf16[64,256]{1,0:T(8,128)(2,1)S(1)}, u32[]{:S(2)}, u32[]{:S(2)}) %collective-permute-start) | collective-permute-done | bytes 32800 | tf_op jit(solution)/shard_map/ppermute | solution.py:200
  46.2 4.4 %collective-permute-start.5 = (bf16[256,256]{1,0:T(8,128)(2,1)S(1)}, bf16[256,256]{1,0:T(8,128)(2,1)S(1)}, u32[]{:S(2)}, u32[]{:S(2)}) collective-permute-start(bf16[256,256]{1,0:T(8,128)(2,1)S(1)} %constant_dynamic-update-slice_fusion.rest_0_), channel_id=1, source_target_pairs={{0,48},{16,32},{32,16},{48,0},{1,49},{17,33},{33,17},{49,1},{2,50}... | collective-permute-start | bytes 393224 | tf_op jit(solution)/shard_map/ppermute | solution.py:200
  50.6 2.4 %collective-permute-start.4 = (bf16[256,256]{1,0:T(8,128)(2,1)S(1)}, bf16[256,256]{1,0:T(8,128)(2,1)S(1)}, u32[]{:S(2)}, u32[]{:S(2)}) collective-permute-start(bf16[256,256]{1,0:T(8,128)(2,1)S(1)} %constant_dynamic-update-slice_fusion.rest_0_), channel_id=1, source_target_pairs={{0,32},{16,48},{32,0},{48,16},{1,33},{17,49},{33,1},{49,17},{2,34}... | collective-permute-start | bytes 393224 | tf_op jit(solution)/shard_map/ppermute | solution.py:200
  53.1 2.2 %collective-permute-start.3 = (bf16[256,256]{1,0:T(8,128)(2,1)S(1)}, bf16[256,256]{1,0:T(8,128)(2,1)S(1)}, u32[]{:S(2)}, u32[]{:S(2)}) collective-permute-start(bf16[256,256]{1,0:T(8,128)(2,1)S(1)} %constant_dynamic-update-slice_fusion.rest_0_), channel_id=1, source_target_pairs={{0,16},{16,0},{32,48},{48,32},{1,17},{17,1},{33,49},{49,33},{2,18}... | collective-permute-start | bytes 393224 | tf_op jit(solution)/shard_map/ppermute | solution.py:200
  55.3 2.6 %collective-permute-done.4.rest_2_ = bf16[256,256]{1,0:T(8,128)(2,1)S(1)} collective-permute-done((bf16[256,256]{1,0:T(8,128)(2,1)S(1)}, bf16[256,256]{1,0:T(8,128)(2,1)S(1)}, u32[]{:S(2)}, u32[]{:S(2)}) %collective-permute-start.4) | collective-permute-done | bytes 131104 | tf_op jit(solution)/shard_map/ppermute | solution.py:200
  57.9 1.5 %collective-permute-done.3.rest_1_ = bf16[256,256]{1,0:T(8,128)(2,1)S(1)} collective-permute-done((bf16[256,256]{1,0:T(8,128)(2,1)S(1)}, bf16[256,256]{1,0:T(8,128)(2,1)S(1)}, u32[]{:S(2)}, u32[]{:S(2)}) %collective-permute-start.3) | collective-permute-done | bytes 131104 | tf_op jit(solution)/shard_map/ppermute | solution.py:200
  59.3 4.5 %all-to-all-done.1.blocks = bf16[8,32,2304]{2,1,0:T(8,128)(2,1)S(1)} async-done(((bf16[8,32,2304]{2,1,0:T(8,128)(2,1)}), bf16[8,32,2304]{2,1,0:T(8,128)(2,1)S(1)}, u32[]{:S(2)}, u32[]{:S(2)}) %all-to-all-start.1) | async-done | bytes 1179680 | tf_op jit(solution)/shard_map/all_to_all | solution.py:260
  63.8 13.1 %attend.1 = (bf16[8,32,2304]{2,1,0:T(8,128)(2,1)}, bf16[256,256]{1,0:T(8,128)(2,1)S(1)}, bf16[256,256]{1,0:T(8,128)(2,1)S(1)}, bf16[256,256]{1,0:T(8,128)(2,1)S(1)}, bf16[256,256]{1,0:T(8,128)(2,1)S(1)}) custom-call(s32[1,4]{1,0:T(1,128)S(1)} %copy-done, bf16[8,32,2304]{2,1,0:T(8,128)(2,1)S(1)} %all-to-all-done.1.blocks, ...), custom_call_target="tpu_custom_call" | custom-call | flops 4026531840 | bytes 4194304 | tf_op jit(solution)/shard_map/attend/pallas_call | solution.py:207
  77.0 4.3 %all-to-all-start.2 = ((bf16[8,32,2304]{2,1,0:T(8,128)(2,1)}), bf16[8,32,2304]{2,1,0:T(8,128)(2,1)S(1)}, u32[]{:S(2)}, u32[]{:S(2)}) async-start(bf16[8,32,2304]{2,1,0:T(8,128)(2,1)} %get-tuple-element.25), calls=%async_computation.2 | async-start | bytes 2359296 | tf_op jit(solution)/shard_map/all_to_all | solution.py:268
  81.3 3.1 %collective-permute-start.6 = (bf16[256,256]{1,0:T(8,128)(2,1)S(1)}, bf16[256,256]{1,0:T(8,128)(2,1)S(1)}, u32[]{:S(2)}, u32[]{:S(2)}) collective-permute-start(bf16[256,256]{1,0:T(8,128)(2,1)S(1)} %get-tuple-element.22), channel_id=1, source_target_pairs={{0,16},{16,0},{32,48},{48,32},{1,17},{17,1},{33,49},{49,33},{2,18}... | collective-permute-start | bytes 393224 | tf_op jit(solution)/shard_map/ppermute | solution.py:200
  84.5 4.4 %collective-permute-start.7 = (bf16[256,256]{1,0:T(8,128)(2,1)S(1)}, bf16[256,256]{1,0:T(8,128)(2,1)S(1)}, u32[]{:S(2)}, u32[]{:S(2)}) collective-permute-start(bf16[256,256]{1,0:T(8,128)(2,1)S(1)} %get-tuple-element.23), channel_id=1, source_target_pairs={{0,32},{16,48},{32,0},{48,16},{1,33},{17,49},{33,1},{49,17},{2,34}... | collective-permute-start | bytes 393224 | tf_op jit(solution)/shard_map/ppermute | solution.py:200
  88.8 2.1 %collective-permute-start.8 = (bf16[256,256]{1,0:T(8,128)(2,1)S(1)}, bf16[256,256]{1,0:T(8,128)(2,1)S(1)}, u32[]{:S(2)}, u32[]{:S(2)}) collective-permute-start(bf16[256,256]{1,0:T(8,128)(2,1)S(1)} %get-tuple-element.24), channel_id=1, source_target_pairs={{0,48},{16,32},{32,16},{48,0},{1,49},{17,33},{33,17},{49,1},{2,50}... | collective-permute-start | bytes 393224 | tf_op jit(solution)/shard_map/ppermute | solution.py:200
  90.9 2.3 %collective-permute-done.7 = bf16[256,256]{1,0:T(8,128)(2,1)S(1)} collective-permute-done((bf16[256,256]{1,0:T(8,128)(2,1)S(1)}, bf16[256,256]{1,0:T(8,128)(2,1)S(1)}, u32[]{:S(2)}, u32[]{:S(2)}) %collective-permute-start.7) | collective-permute-done | bytes 131104 | tf_op jit(solution)/shard_map/ppermute | solution.py:200
  93.2 3.0 %collective-permute-done.8 = bf16[256,256]{1,0:T(8,128)(2,1)S(1)} collective-permute-done((bf16[256,256]{1,0:T(8,128)(2,1)S(1)}, bf16[256,256]{1,0:T(8,128)(2,1)S(1)}, u32[]{:S(2)}, u32[]{:S(2)}) %collective-permute-start.8) | collective-permute-done | bytes 131104 | tf_op jit(solution)/shard_map/ppermute | solution.py:200
  96.3 2.3 %collective-permute-start.9 = (bf16[64,256]{1,0:T(8,128)(2,1)S(1)}, bf16[64,256]{1,0:T(8,128)(2,1)S(1)}, u32[]{:S(2)}, u32[]{:S(2)}) collective-permute-start(bf16[64,256]{1,0:T(8,128)(2,1)S(1)} %get-tuple-element.32), channel_id=1, source_target_pairs={{0,64},{64,0},{128,192},{192,128},{1,65},{65,1},{129,193},{193,129... | collective-permute-start | bytes 98312 | tf_op jit(solution)/shard_map/ppermute | solution.py:200
  98.7 3.2 %collective-permute-start.11 = (bf16[64,256]{1,0:T(8,128)(2,1)S(1)}, bf16[64,256]{1,0:T(8,128)(2,1)S(1)}, u32[]{:S(2)}, u32[]{:S(2)}) collective-permute-start(bf16[64,256]{1,0:T(8,128)(2,1)S(1)} %get-tuple-element.33), channel_id=1, source_target_pairs={{0,192},{64,128},{128,64},{192,0},{1,193},{65,129},{129,65},{193,1... | collective-permute-start | bytes 98312 | tf_op jit(solution)/shard_map/ppermute | solution.py:200
  101.9 2.9 %collective-permute-start.10 = (bf16[64,256]{1,0:T(8,128)(2,1)S(1)}, bf16[64,256]{1,0:T(8,128)(2,1)S(1)}, u32[]{:S(2)}, u32[]{:S(2)}) collective-permute-start(bf16[64,256]{1,0:T(8,128)(2,1)S(1)} %get-tuple-element.34), channel_id=1, source_target_pairs={{0,128},{64,192},{128,0},{192,64},{1,129},{65,193},{129,1},{193,65... | collective-permute-start | bytes 98312 | tf_op jit(solution)/shard_map/ppermute | solution.py:200
  105.1 3.0 %collective-permute-done.10 = bf16[64,256]{1,0:T(8,128)(2,1)S(1)} collective-permute-done((bf16[64,256]{1,0:T(8,128)(2,1)S(1)}, bf16[64,256]{1,0:T(8,128)(2,1)S(1)}, u32[]{:S(2)}, u32[]{:S(2)}) %collective-permute-start.10) | collective-permute-done | bytes 32800 | tf_op jit(solution)/shard_map/ppermute | solution.py:200
  108.1 1.8 %all-to-all-done.2.blocks = bf16[8,32,2304]{2,1,0:T(8,128)(2,1)S(1)} async-done(((bf16[8,32,2304]{2,1,0:T(8,128)(2,1)}), bf16[8,32,2304]{2,1,0:T(8,128)(2,1)S(1)}, u32[]{:S(2)}, u32[]{:S(2)}) %all-to-all-start.2) | async-done | bytes 1179680 | tf_op jit(solution)/shard_map/all_to_all | solution.py:268
  109.9 0.7 reshape.49
  110.6 5.8 %all-to-all-start.3 = ((f32[32,2,256]{2,1,0:T(2,128)}), f32[32,2,256]{2,1,0:T(2,128)S(1)}, u32[]{:S(2)}, u32[]{:S(2)}) async-start(f32[32,2,256]{2,1,0:T(2,128)} %reshape.49), calls=%async_computation.3 | async-start | bytes 131072 | tf_op jit(solution)/shard_map/all_to_all | solution.py:279
  116.4 2.6 %unpack.1 = (bf16[32,8192]{1,0:T(8,128)(2,1)}, bf16[32,8192]{1,0:T(8,128)(2,1)}, bf16[32,1024]{1,0:T(8,128)(2,1)}, bf16[32,1024]{1,0:T(8,128)(2,1)}) custom-call(bf16[8,32,2304]{2,1,0:T(8,128)(2,1)} %copy-done.1), custom_call_target="tpu_custom_call" | custom-call | tf_op jit(solution)/shard_map/unpack/pallas_call | solution.py:285
  119.1 9.2 %all-to-all-done.3 = f32[32,2,256]{2,1,0:T(2,128)S(1)} async-done(((f32[32,2,256]{2,1,0:T(2,128)}), f32[32,2,256]{2,1,0:T(2,128)S(1)}, u32[]{:S(2)}, u32[]{:S(2)}) %all-to-all-start.3) | async-done | bytes 65568 | tf_op jit(solution)/shard_map/all_to_all | solution.py:279
  (23 shorter events, 1.3 us)
Async XLA Ops:
  2.0 29.0 %all-to-all-start = ((bf16[32,2,256]{2,1,0:T(2,128)(2,1)}), bf16[32,2,256]{2,1,0:T(2,128)(2,1)S(1)}, u32[]{:S(2)}, u32[]{:S(2)}) async-start(bf16[32,2,256]{2,1,0:T(2,128)(2,1)} %bitcast.1), calls=%async_computation | async-start | bytes 65536 | tf_op jit(solution)/shard_map/all_to_all | solution.py:249
  21.9 41.9 %copy-start = (s32[1,4]{1,0:T(1,128)S(1)}, s32[1,4]{1,0:T(1,128)}, u32[]{:S(2)}) copy-start(s32[1,4]{1,0:T(1,128)} %len_ref.1) | copy-start | bytes 52
  31.0 32.8 %all-to-all-start.1 = ((bf16[8,32,2304]{2,1,0:T(8,128)(2,1)}), bf16[8,32,2304]{2,1,0:T(8,128)(2,1)S(1)}, u32[]{:S(2)}, u32[]{:S(2)}) async-start(bf16[8,32,2304]{2,1,0:T(8,128)(2,1)} %pack.1), calls=%async_computation.1 | async-start | bytes 2359296 | tf_op jit(solution)/shard_map/all_to_all | solution.py:260
  35.3 10.9 %collective-permute-start.2 = (bf16[64,256]{1,0:T(8,128)(2,1)S(1)}, bf16[64,256]{1,0:T(8,128)(2,1)S(1)}, u32[]{:S(2)}, u32[]{:S(2)}) collective-permute-start(bf16[64,256]{1,0:T(8,128)(2,1)S(1)} %reshape.48), channel_id=1, source_target_pairs={{0,192},{64,128},{128,64},{192,0},{1,193},{65,129},{129,65},{193,1... | collective-permute-start | bytes 98312 | tf_op jit(solution)/shard_map/ppermute | solution.py:200
  37.9 8.3 %collective-permute-start.1 = (bf16[64,256]{1,0:T(8,128)(2,1)S(1)}, bf16[64,256]{1,0:T(8,128)(2,1)S(1)}, u32[]{:S(2)}, u32[]{:S(2)}) collective-permute-start(bf16[64,256]{1,0:T(8,128)(2,1)S(1)} %reshape.48), channel_id=1, source_target_pairs={{0,128},{64,192},{128,0},{192,64},{1,129},{65,193},{129,1},{193,65... | collective-permute-start | bytes 98312 | tf_op jit(solution)/shard_map/ppermute | solution.py:200
  40.7 5.5 %collective-permute-start = (bf16[64,256]{1,0:T(8,128)(2,1)S(1)}, bf16[64,256]{1,0:T(8,128)(2,1)S(1)}, u32[]{:S(2)}, u32[]{:S(2)}) collective-permute-start(bf16[64,256]{1,0:T(8,128)(2,1)S(1)} %reshape.48), channel_id=1, source_target_pairs={{0,64},{64,0},{128,192},{192,128},{1,65},{65,1},{129,193},{193,129... | collective-permute-start | bytes 98312 | tf_op jit(solution)/shard_map/ppermute | solution.py:200
  46.2 9.0 %collective-permute-start.5 = (bf16[256,256]{1,0:T(8,128)(2,1)S(1)}, bf16[256,256]{1,0:T(8,128)(2,1)S(1)}, u32[]{:S(2)}, u32[]{:S(2)}) collective-permute-start(bf16[256,256]{1,0:T(8,128)(2,1)S(1)} %constant_dynamic-update-slice_fusion.rest_0_), channel_id=1, source_target_pairs={{0,48},{16,32},{32,16},{48,0},{1,49},{17,33},{33,17},{49,1},{2,50}... | collective-permute-start | bytes 393224 | tf_op jit(solution)/shard_map/ppermute | solution.py:200
  50.6 7.2 %collective-permute-start.4 = (bf16[256,256]{1,0:T(8,128)(2,1)S(1)}, bf16[256,256]{1,0:T(8,128)(2,1)S(1)}, u32[]{:S(2)}, u32[]{:S(2)}) collective-permute-start(bf16[256,256]{1,0:T(8,128)(2,1)S(1)} %constant_dynamic-update-slice_fusion.rest_0_), channel_id=1, source_target_pairs={{0,32},{16,48},{32,0},{48,16},{1,33},{17,49},{33,1},{49,17},{2,34}... | collective-permute-start | bytes 393224 | tf_op jit(solution)/shard_map/ppermute | solution.py:200
  53.1 6.2 %collective-permute-start.3 = (bf16[256,256]{1,0:T(8,128)(2,1)S(1)}, bf16[256,256]{1,0:T(8,128)(2,1)S(1)}, u32[]{:S(2)}, u32[]{:S(2)}) collective-permute-start(bf16[256,256]{1,0:T(8,128)(2,1)S(1)} %constant_dynamic-update-slice_fusion.rest_0_), channel_id=1, source_target_pairs={{0,16},{16,0},{32,48},{48,32},{1,17},{17,1},{33,49},{49,33},{2,18}... | collective-permute-start | bytes 393224 | tf_op jit(solution)/shard_map/ppermute | solution.py:200
  77.0 32.9 %all-to-all-start.2 = ((bf16[8,32,2304]{2,1,0:T(8,128)(2,1)}), bf16[8,32,2304]{2,1,0:T(8,128)(2,1)S(1)}, u32[]{:S(2)}, u32[]{:S(2)}) async-start(bf16[8,32,2304]{2,1,0:T(8,128)(2,1)} %get-tuple-element.25), calls=%async_computation.2 | async-start | bytes 2359296 | tf_op jit(solution)/shard_map/all_to_all | solution.py:268
  81.3 9.6 %collective-permute-start.6 = (bf16[256,256]{1,0:T(8,128)(2,1)S(1)}, bf16[256,256]{1,0:T(8,128)(2,1)S(1)}, u32[]{:S(2)}, u32[]{:S(2)}) collective-permute-start(bf16[256,256]{1,0:T(8,128)(2,1)S(1)} %get-tuple-element.22), channel_id=1, source_target_pairs={{0,16},{16,0},{32,48},{48,32},{1,17},{17,1},{33,49},{49,33},{2,18}... | collective-permute-start | bytes 393224 | tf_op jit(solution)/shard_map/ppermute | solution.py:200
  84.5 8.8 %collective-permute-start.7 = (bf16[256,256]{1,0:T(8,128)(2,1)S(1)}, bf16[256,256]{1,0:T(8,128)(2,1)S(1)}, u32[]{:S(2)}, u32[]{:S(2)}) collective-permute-start(bf16[256,256]{1,0:T(8,128)(2,1)S(1)} %get-tuple-element.23), channel_id=1, source_target_pairs={{0,32},{16,48},{32,0},{48,16},{1,33},{17,49},{33,1},{49,17},{2,34}... | collective-permute-start | bytes 393224 | tf_op jit(solution)/shard_map/ppermute | solution.py:200
  88.8 7.4 %collective-permute-start.8 = (bf16[256,256]{1,0:T(8,128)(2,1)S(1)}, bf16[256,256]{1,0:T(8,128)(2,1)S(1)}, u32[]{:S(2)}, u32[]{:S(2)}) collective-permute-start(bf16[256,256]{1,0:T(8,128)(2,1)S(1)} %get-tuple-element.24), channel_id=1, source_target_pairs={{0,48},{16,32},{32,16},{48,0},{1,49},{17,33},{33,17},{49,1},{2,50}... | collective-permute-start | bytes 393224 | tf_op jit(solution)/shard_map/ppermute | solution.py:200
  96.3 8.4 %collective-permute-start.9 = (bf16[64,256]{1,0:T(8,128)(2,1)S(1)}, bf16[64,256]{1,0:T(8,128)(2,1)S(1)}, u32[]{:S(2)}, u32[]{:S(2)}) collective-permute-start(bf16[64,256]{1,0:T(8,128)(2,1)S(1)} %get-tuple-element.32), channel_id=1, source_target_pairs={{0,64},{64,0},{128,192},{192,128},{1,65},{65,1},{129,193},{193,129... | collective-permute-start | bytes 98312 | tf_op jit(solution)/shard_map/ppermute | solution.py:200
  98.7 6.5 %collective-permute-start.11 = (bf16[64,256]{1,0:T(8,128)(2,1)S(1)}, bf16[64,256]{1,0:T(8,128)(2,1)S(1)}, u32[]{:S(2)}, u32[]{:S(2)}) collective-permute-start(bf16[64,256]{1,0:T(8,128)(2,1)S(1)} %get-tuple-element.33), channel_id=1, source_target_pairs={{0,192},{64,128},{128,64},{192,0},{1,193},{65,129},{129,65},{193,1... | collective-permute-start | bytes 98312 | tf_op jit(solution)/shard_map/ppermute | solution.py:200
  101.9 6.2 %collective-permute-start.10 = (bf16[64,256]{1,0:T(8,128)(2,1)S(1)}, bf16[64,256]{1,0:T(8,128)(2,1)S(1)}, u32[]{:S(2)}, u32[]{:S(2)}) collective-permute-start(bf16[64,256]{1,0:T(8,128)(2,1)S(1)} %get-tuple-element.34), channel_id=1, source_target_pairs={{0,128},{64,192},{128,0},{192,64},{1,129},{65,193},{129,1},{193,65... | collective-permute-start | bytes 98312 | tf_op jit(solution)/shard_map/ppermute | solution.py:200
  109.9 6.5 %copy-start.1 = (bf16[8,32,2304]{2,1,0:T(8,128)(2,1)}, bf16[8,32,2304]{2,1,0:T(8,128)(2,1)S(1)}, u32[]{:S(2)}) copy-start(bf16[8,32,2304]{2,1,0:T(8,128)(2,1)S(1)} %all-to-all-done.2.blocks) | copy-start | bytes 3538948
  110.6 17.6 %all-to-all-start.3 = ((f32[32,2,256]{2,1,0:T(2,128)}), f32[32,2,256]{2,1,0:T(2,128)S(1)}, u32[]{:S(2)}, u32[]{:S(2)}) async-start(f32[32,2,256]{2,1,0:T(2,128)} %reshape.49), calls=%async_computation.3 | async-start | bytes 131072 | tf_op jit(solution)/shard_map/all_to_all | solution.py:279

commit v3 on v2

--- a/solution.py
+++ b/solution.py
@@ -9,7 +9,7 @@
 from jax.sharding import Mesh, PartitionSpec as P
 
 DH = 128
-AXES = ("y_hi", "y_lo", "x", "z_hi", "z_lo", "core")
+AXES = ("y_lo", "y_hi", "x", "z_hi", "z_lo", "core")
 FIRST_AXES = ("y_hi", "z_hi", "z_lo", "core")
 HEAD_AXES = ("z_lo", "core")
 PEERS = 8
@@ -104,7 +104,6 @@
         ends.append(total)
     lanes = lax.broadcasted_iota(jnp.int32, (1, WIDTH), 1)
     key_at = lax.broadcasted_iota(jnp.int32, (STEP, WIDTH), 0)
-    chunks = [slice(c * CHUNK, (c + 1) * CHUNK) for c in range(KEYS // CHUNK)]
     steps = [slice(c * STEP, (c + 1) * STEP) for c in range(KEYS // STEP)]
 
     def stacked(s, base):
@@ -144,12 +143,11 @@
         factors = [factor * inverse for factor in factors]
         for c, factor in zip(steps, factors):
             p_ref[c, :] = (e_ref[c, :] * factor).astype(jnp.bfloat16)
-        for c in chunks:
-            part = jnp.dot(p_ref[c, :], g, preferred_element_type=jnp.float32)
-            if s == 0:
-                dvalues[c, :] = part
-            else:
-                dvalues[c, :] += part
+        part = jnp.dot(p_ref[...], g, preferred_element_type=jnp.float32)
+        if s == 0:
+            dvalues[...] = part
+        else:
+            dvalues[...] += part
         out_t = jnp.dot(values_t[...], p_ref[...], preferred_element_type=jnp.float32)
         out_t = out_t.astype(jnp.bfloat16)
         delta = jnp.sum(
@@ -158,12 +156,11 @@
         for c, factor in zip(steps, factors):
             dw = jnp.dot(values[c, :], g_t, preferred_element_type=jnp.float32)
             d_ref[c, :] = ((e_ref[c, :] * factor) * (dw - delta)).astype(jnp.bfloat16)
-        for c in chunks:
-            part = jnp.dot(d_ref[c, :], q, preferred_element_type=jnp.float32)
-            if s == 0:
-                dkeys[c, :] = part
-            else:
-                dkeys[c, :] += part
+        part = jnp.dot(d_ref[...], q, preferred_element_type=jnp.float32)
+        if s == 0:
+            dkeys[...] = part
+        else:
+            dkeys[...] += part
         dq_t = jnp.dot(keys_t[...], d_ref[...], preferred_element_type=jnp.float32) * SCALE
         out = out_t.T
         dq = dq_t.astype(jnp.bfloat16).T
@@ -275,10 +272,8 @@
     total = pieces[0].astype(f32)
     for b in (1, 2, 3):
         total = total + across(pieces[b], "y_lo", b).astype(f32)
-    total, back = lax.optimization_barrier((total, back))
-    owned = lax.all_to_all(
-        total.reshape(FIRST, own_rows, 2 * DH), FIRST_AXES, split_axis=0, concat_axis=0, tiled=True
-    )
+    total, back = lax.optimization_barrier((total.reshape(FIRST, own_rows, 2 * DH), back))
+    owned = lax.all_to_all(total, FIRST_AXES, split_axis=0, concat_axis=0, tiled=True)
     owned = jnp.sum(owned.reshape(4, PEERS, own_rows, 2, DH), axis=0)
     owned = owned.transpose(2, 1, 0, 3).reshape(2, own_rows, PEERS * DH)
 
@@ -294,12 +289,12 @@
 
 
 def solution(mesh):
-    fine = Mesh(mesh.devices.reshape(2, 4, 4, 2, 4, 2), AXES)
+    fine = Mesh(mesh.devices.reshape(4, 2, 4, 2, 4, 2), AXES)
     rows = P(AXES, None)
     return jax.shard_map(
         on_device,
         mesh=fine,
-        in_specs=(rows,) * 6 + (P(("y_hi", "y_lo", "x", "z_hi"), None),),
+        in_specs=(rows,) * 6 + (P(("y_lo", "y_hi", "x", "z_hi"), None),),
         out_specs=(rows,) * 6,
         check_vma=False,
     )

time: 130 us -> 125 us (0.962)
  waiting for transfers between devices: 38.9 us -> 28.3 us
  starting transfers between devices: 67.9 us -> 74 us
    ppermute x12, starting transfers between devices: 36.2 us -> 41.3 us  [across(): return lax.ppermute(value, axis, [(i, i ^ s) for i in range(n)])]
    all_to_all x1, waiting for transfers between devices: 4.52 us -> 0.01 us  [on_device(): lax.all_to_all(packed, HEAD_AXES, split_axis=0, concat_axis=0, tiled=True)]
    all_to_all x1, starting transfers between devices: 17.2 us -> 13 us  [on_device(): lax.all_to_all(by_head, FIRST_AXES, split_axis=0, concat_axis=0, tiled=True)]
    all_to_all x1, waiting for transfers between devices: 9.19 us -> 5.28 us  [on_device(): lax.all_to_all(total, FIRST_AXES, split_axis=0, concat_axis=0, tiled=True)]
    all_to_all x1, waiting for transfers between devices: 9.09 us -> 5.18 us  [on_device(): lax.all_to_all(by_head, FIRST_AXES, split_axis=0, concat_axis=0, tiled=True)]
    ppermute x12, waiting for transfers between devices: 14.3 us -> 17.8 us  [across(): return lax.ppermute(value, axis, [(i, i ^ s) for i in range(n)])]
    all_to_all x1, starting transfers between devices: 4.35 us -> 7.43 us  [on_device(): lax.all_to_all(made, HEAD_AXES, split_axis=0, concat_axis=0, tiled=True)]
    all_to_all x1, starting transfers between devices: 5.8 us -> 8.03 us  [on_device(): lax.all_to_all(total, FIRST_AXES, split_axis=0, concat_axis=0, tiled=True)]
  transfers between devices with their start and end apart: 16 -> 16, of which waited for: 11 -> 8; matrix products, arithmetic and copies ran while one was open for 0% -> 1% of each run, Pallas kernels for 4% -> 4%
where the time goes in v3:
time: 125 us; the launch traced here: 124 us
  starting transfers between devices  74 us (59%)
  waiting for transfers between devices  28.3 us (23%)
  Pallas kernels  18.1 us (14%)
  local copies, waits for them, and re-layouts  2.76 us (2%)
    ppermute x12, starting transfers between devices, across(): return lax.ppermute(value, axis, [(i, i ^ s) for i in range(n)])  41.3 us
    ppermute x12, waiting for transfers between devices, across(): return lax.ppermute(value, axis, [(i, i ^ s) for i in range(n)])  17.8 us
    all_to_all x1, starting transfers between devices, on_device(): lax.all_to_all(by_head, FIRST_AXES, split_axis=0, concat_axis=0, tiled=True)  13 us
    pallas_call x1, Pallas kernels, attend(): pl.pallas_call(attend_kernel, out_shape=[block] + [piece] * XS, in_specs=...  12.8 us
    all_to_all x1, starting transfers between devices, on_device(): lax.all_to_all(total, FIRST_AXES, split_axis=0, concat_axis=0, tiled=True)  8.03 us
    all_to_all x1, starting transfers between devices, on_device(): lax.all_to_all(made, HEAD_AXES, split_axis=0, concat_axis=0, tiled=True)  7.43 us
    all_to_all x1, waiting for transfers between devices, on_device(): lax.all_to_all(total, FIRST_AXES, split_axis=0, concat_axis=0, tiled=True)  5.28 us
    all_to_all x1, waiting for transfers between devices, on_device(): lax.all_to_all(by_head, FIRST_AXES, split_axis=0, concat_axis=0, tiled=True)  5.18 us
  transfers between devices with their start and end apart: 16, of which 8 were waited for; matrix products, arithmetic and copies ran while one was open for 1% of the time, Pallas kernels for 4%

profile of v3, /device:TPU:1, one launch (start us, length us, event | category | flops | bytes accessed | tf_op | source)
XLA Modules:
  0.0 124.2 jit_solution(7482809319652154967)
XLA Ops:
  0.6 0.7 copy_bitcast_fusion
  1.4 0.6 broadcast_in_dim.2
  2.0 13.0 %all-to-all-start = ((bf16[32,2,256]{2,1,0:T(2,128)(2,1)}), bf16[32,2,256]{2,1,0:T(2,128)(2,1)S(1)}, u32[]{:S(2)}, u32[]{:S(2)}) async-start(bf16[32,2,256]{2,1,0:T(2,128)(2,1)} %bitcast.1), calls=%async_computation | async-start | bytes 65536 | tf_op jit(solution)/shard_map/all_to_all | solution.py:246
  15.0 2.7 %pack.1 = bf16[8,32,2304]{2,1,0:T(8,128)(2,1)} custom-call(bf16[32,8192]{1,0:T(8,128)(2,1)} %q_ref.1, bf16[32,8192]{1,0:T(8,128)(2,1)} %g_ref.1, bf16[32,1024]{1,0:T(8,128)(2,1)} %k_ref.1, bf16[32,1024]{1,0:T(8,128)(2,1)} %v_ref.1), custom_call_target="tpu_custom_call" | custom-call | tf_op jit(solution)/shard_map/pack/pallas_call | solution.py:248
  17.7 5.2 %all-to-all-done = bf16[32,2,256]{2,1,0:T(2,128)(2,1)S(1)} async-done(((bf16[32,2,256]{2,1,0:T(2,128)(2,1)}), bf16[32,2,256]{2,1,0:T(2,128)(2,1)S(1)}, u32[]{:S(2)}, u32[]{:S(2)}) %all-to-all-start) | async-done | bytes 32800 | tf_op jit(solution)/shard_map/all_to_all | solution.py:246
  22.9 4.3 %all-to-all-start.1 = ((bf16[8,32,2304]{2,1,0:T(8,128)(2,1)}), bf16[8,32,2304]{2,1,0:T(8,128)(2,1)S(1)}, u32[]{:S(2)}, u32[]{:S(2)}) async-start(bf16[8,32,2304]{2,1,0:T(8,128)(2,1)} %pack.1), calls=%async_computation.1 | async-start | bytes 2359296 | tf_op jit(solution)/shard_map/all_to_all | solution.py:257
  27.1 5.0 %collective-permute-start.2 = (bf16[64,256]{1,0:T(8,128)(2,1)S(1)}, bf16[64,256]{1,0:T(8,128)(2,1)S(1)}, u32[]{:S(2)}, u32[]{:S(2)}) collective-permute-start(bf16[64,256]{1,0:T(8,128)(2,1)S(1)} %reshape.48), channel_id=1, source_target_pairs={{0,384},{128,256},{256,128},{384,0},{1,385},{129,257},{257,129},{3... | collective-permute-start | bytes 98312 | tf_op jit(solution)/shard_map/ppermute | solution.py:197
  32.2 4.4 %collective-permute-start.1 = (bf16[64,256]{1,0:T(8,128)(2,1)S(1)}, bf16[64,256]{1,0:T(8,128)(2,1)S(1)}, u32[]{:S(2)}, u32[]{:S(2)}) collective-permute-start(bf16[64,256]{1,0:T(8,128)(2,1)S(1)} %reshape.48), channel_id=1, source_target_pairs={{0,256},{128,384},{256,0},{384,128},{1,257},{129,385},{257,1},{385... | collective-permute-start | bytes 98312 | tf_op jit(solution)/shard_map/ppermute | solution.py:197
  36.6 2.0 %collective-permute-start = (bf16[64,256]{1,0:T(8,128)(2,1)S(1)}, bf16[64,256]{1,0:T(8,128)(2,1)S(1)}, u32[]{:S(2)}, u32[]{:S(2)}) collective-permute-start(bf16[64,256]{1,0:T(8,128)(2,1)S(1)} %reshape.48), channel_id=1, source_target_pairs={{0,128},{128,0},{256,384},{384,256},{1,129},{129,1},{257,385},{385... | collective-permute-start | bytes 98312 | tf_op jit(solution)/shard_map/ppermute | solution.py:197
  38.6 4.2 %collective-permute-done = bf16[64,256]{1,0:T(8,128)(2,1)S(1)} collective-permute-done((bf16[64,256]{1,0:T(8,128)(2,1)S(1)}, bf16[64,256]{1,0:T(8,128)(2,1)S(1)}, u32[]{:S(2)}, u32[]{:S(2)}) %collective-permute-start) | collective-permute-done | bytes 32800 | tf_op jit(solution)/shard_map/ppermute | solution.py:197
  42.8 4.4 %collective-permute-start.5 = (bf16[256,256]{1,0:T(8,128)(2,1)S(1)}, bf16[256,256]{1,0:T(8,128)(2,1)S(1)}, u32[]{:S(2)}, u32[]{:S(2)}) collective-permute-start(bf16[256,256]{1,0:T(8,128)(2,1)S(1)} %constant_dynamic-update-slice_fusion.rest_0_), channel_id=1, source_target_pairs={{0,48},{16,32},{32,16},{48,0},{1,49},{17,33},{33,17},{49,1},{2,50}... | collective-permute-start | bytes 393224 | tf_op jit(solution)/shard_map/ppermute | solution.py:197
  47.2 2.4 %collective-permute-start.4 = (bf16[256,256]{1,0:T(8,128)(2,1)S(1)}, bf16[256,256]{1,0:T(8,128)(2,1)S(1)}, u32[]{:S(2)}, u32[]{:S(2)}) collective-permute-start(bf16[256,256]{1,0:T(8,128)(2,1)S(1)} %constant_dynamic-update-slice_fusion.rest_0_), channel_id=1, source_target_pairs={{0,32},{16,48},{32,0},{48,16},{1,33},{17,49},{33,1},{49,17},{2,34}... | collective-permute-start | bytes 393224 | tf_op jit(solution)/shard_map/ppermute | solution.py:197
  49.7 2.2 %collective-permute-start.3 = (bf16[256,256]{1,0:T(8,128)(2,1)S(1)}, bf16[256,256]{1,0:T(8,128)(2,1)S(1)}, u32[]{:S(2)}, u32[]{:S(2)}) collective-permute-start(bf16[256,256]{1,0:T(8,128)(2,1)S(1)} %constant_dynamic-update-slice_fusion.rest_0_), channel_id=1, source_target_pairs={{0,16},{16,0},{32,48},{48,32},{1,17},{17,1},{33,49},{49,33},{2,18}... | collective-permute-start | bytes 393224 | tf_op jit(solution)/shard_map/ppermute | solution.py:197
  51.9 2.6 %collective-permute-done.4.rest_2_ = bf16[256,256]{1,0:T(8,128)(2,1)S(1)} collective-permute-done((bf16[256,256]{1,0:T(8,128)(2,1)S(1)}, bf16[256,256]{1,0:T(8,128)(2,1)S(1)}, u32[]{:S(2)}, u32[]{:S(2)}) %collective-permute-start.4) | collective-permute-done | bytes 131104 | tf_op jit(solution)/shard_map/ppermute | solution.py:197
  54.5 1.7 %collective-permute-done.3.rest_1_ = bf16[256,256]{1,0:T(8,128)(2,1)S(1)} collective-permute-done((bf16[256,256]{1,0:T(8,128)(2,1)S(1)}, bf16[256,256]{1,0:T(8,128)(2,1)S(1)}, u32[]{:S(2)}, u32[]{:S(2)}) %collective-permute-start.3) | collective-permute-done | bytes 131104 | tf_op jit(solution)/shard_map/ppermute | solution.py:197
  56.2 12.8 %attend.1 = (bf16[8,32,2304]{2,1,0:T(8,128)(2,1)}, bf16[256,256]{1,0:T(8,128)(2,1)S(1)}, bf16[256,256]{1,0:T(8,128)(2,1)S(1)}, bf16[256,256]{1,0:T(8,128)(2,1)S(1)}, bf16[256,256]{1,0:T(8,128)(2,1)S(1)}) custom-call(s32[1,4]{1,0:T(1,128)S(1)} %copy-done, bf16[8,32,2304]{2,1,0:T(8,128)(2,1)S(1)} %all-to-all-done.1.blocks, ...), custom_call_target="tpu_custom_call" | custom-call | flops 4026531840 | bytes 4194304 | tf_op jit(solution)/shard_map/attend/pallas_call | solution.py:204
  69.0 7.4 %all-to-all-start.2 = ((bf16[8,32,2304]{2,1,0:T(8,128)(2,1)}), bf16[8,32,2304]{2,1,0:T(8,128)(2,1)S(1)}, u32[]{:S(2)}, u32[]{:S(2)}) async-start(bf16[8,32,2304]{2,1,0:T(8,128)(2,1)} %get-tuple-element.25), calls=%async_computation.2 | async-start | bytes 2359296 | tf_op jit(solution)/shard_map/all_to_all | solution.py:265
  76.4 2.2 %collective-permute-start.6 = (bf16[256,256]{1,0:T(8,128)(2,1)S(1)}, bf16[256,256]{1,0:T(8,128)(2,1)S(1)}, u32[]{:S(2)}, u32[]{:S(2)}) collective-permute-start(bf16[256,256]{1,0:T(8,128)(2,1)S(1)} %get-tuple-element.22), channel_id=1, source_target_pairs={{0,16},{16,0},{32,48},{48,32},{1,17},{17,1},{33,49},{49,33},{2,18}... | collective-permute-start | bytes 393224 | tf_op jit(solution)/shard_map/ppermute | solution.py:197
  78.6 4.7 %collective-permute-start.7 = (bf16[256,256]{1,0:T(8,128)(2,1)S(1)}, bf16[256,256]{1,0:T(8,128)(2,1)S(1)}, u32[]{:S(2)}, u32[]{:S(2)}) collective-permute-start(bf16[256,256]{1,0:T(8,128)(2,1)S(1)} %get-tuple-element.23), channel_id=1, source_target_pairs={{0,32},{16,48},{32,0},{48,16},{1,33},{17,49},{33,1},{49,17},{2,34}... | collective-permute-start | bytes 393224 | tf_op jit(solution)/shard_map/ppermute | solution.py:197
  83.2 2.8 %collective-permute-start.8 = (bf16[256,256]{1,0:T(8,128)(2,1)S(1)}, bf16[256,256]{1,0:T(8,128)(2,1)S(1)}, u32[]{:S(2)}, u32[]{:S(2)}) collective-permute-start(bf16[256,256]{1,0:T(8,128)(2,1)S(1)} %get-tuple-element.24), channel_id=1, source_target_pairs={{0,48},{16,32},{32,16},{48,0},{1,49},{17,33},{33,17},{49,1},{2,50}... | collective-permute-start | bytes 393224 | tf_op jit(solution)/shard_map/ppermute | solution.py:197
  86.0 1.7 %collective-permute-done.7 = bf16[256,256]{1,0:T(8,128)(2,1)S(1)} collective-permute-done((bf16[256,256]{1,0:T(8,128)(2,1)S(1)}, bf16[256,256]{1,0:T(8,128)(2,1)S(1)}, u32[]{:S(2)}, u32[]{:S(2)}) %collective-permute-start.7) | collective-permute-done | bytes 131104 | tf_op jit(solution)/shard_map/ppermute | solution.py:197
  87.8 3.1 %collective-permute-done.8 = bf16[256,256]{1,0:T(8,128)(2,1)S(1)} collective-permute-done((bf16[256,256]{1,0:T(8,128)(2,1)S(1)}, bf16[256,256]{1,0:T(8,128)(2,1)S(1)}, u32[]{:S(2)}, u32[]{:S(2)}) %collective-permute-start.8) | collective-permute-done | bytes 131104 | tf_op jit(solution)/shard_map/ppermute | solution.py:197
  90.9 2.0 %collective-permute-start.9 = (bf16[64,256]{1,0:T(8,128)(2,1)S(1)}, bf16[64,256]{1,0:T(8,128)(2,1)S(1)}, u32[]{:S(2)}, u32[]{:S(2)}) collective-permute-start(bf16[64,256]{1,0:T(8,128)(2,1)S(1)} %get-tuple-element.32), channel_id=1, source_target_pairs={{0,128},{128,0},{256,384},{384,256},{1,129},{129,1},{257,385},{385... | collective-permute-start | bytes 98312 | tf_op jit(solution)/shard_map/ppermute | solution.py:197
  92.9 5.0 %collective-permute-start.11 = (bf16[64,256]{1,0:T(8,128)(2,1)S(1)}, bf16[64,256]{1,0:T(8,128)(2,1)S(1)}, u32[]{:S(2)}, u32[]{:S(2)}) collective-permute-start(bf16[64,256]{1,0:T(8,128)(2,1)S(1)} %get-tuple-element.33), channel_id=1, source_target_pairs={{0,384},{128,256},{256,128},{384,0},{1,385},{129,257},{257,129},{3... | collective-permute-start | bytes 98312 | tf_op jit(solution)/shard_map/ppermute | solution.py:197
  97.9 4.4 %collective-permute-start.10 = (bf16[64,256]{1,0:T(8,128)(2,1)S(1)}, bf16[64,256]{1,0:T(8,128)(2,1)S(1)}, u32[]{:S(2)}, u32[]{:S(2)}) collective-permute-start(bf16[64,256]{1,0:T(8,128)(2,1)S(1)} %get-tuple-element.34), channel_id=1, source_target_pairs={{0,256},{128,384},{256,0},{384,128},{1,257},{129,385},{257,1},{385... | collective-permute-start | bytes 98312 | tf_op jit(solution)/shard_map/ppermute | solution.py:197
  102.4 4.5 %collective-permute-done.10 = bf16[64,256]{1,0:T(8,128)(2,1)S(1)} collective-permute-done((bf16[64,256]{1,0:T(8,128)(2,1)S(1)}, bf16[64,256]{1,0:T(8,128)(2,1)S(1)}, u32[]{:S(2)}, u32[]{:S(2)}) %collective-permute-start.10) | collective-permute-done | bytes 32800 | tf_op jit(solution)/shard_map/ppermute | solution.py:197
  106.8 0.7 reshape.49
  107.5 8.0 %all-to-all-start.3 = ((f32[32,2,256]{2,1,0:T(2,128)}), f32[32,2,256]{2,1,0:T(2,128)S(1)}, u32[]{:S(2)}, u32[]{:S(2)}) async-start(f32[32,2,256]{2,1,0:T(2,128)} %reshape.49), calls=%async_computation.3 | async-start | bytes 131072 | tf_op jit(solution)/shard_map/all_to_all | solution.py:276
  115.6 2.6 %unpack.1 = (bf16[32,8192]{1,0:T(8,128)(2,1)}, bf16[32,8192]{1,0:T(8,128)(2,1)}, bf16[32,1024]{1,0:T(8,128)(2,1)}, bf16[32,1024]{1,0:T(8,128)(2,1)}) custom-call(bf16[8,32,2304]{2,1,0:T(8,128)(2,1)} %copy-done.1), custom_call_target="tpu_custom_call" | custom-call | tf_op jit(solution)/shard_map/unpack/pallas_call | solution.py:280
  118.2 5.3 %all-to-all-done.3 = f32[32,2,256]{2,1,0:T(2,128)S(1)} async-done(((f32[32,2,256]{2,1,0:T(2,128)}), f32[32,2,256]{2,1,0:T(2,128)S(1)}, u32[]{:S(2)}, u32[]{:S(2)}) %all-to-all-start.3) | async-done | bytes 65568 | tf_op jit(solution)/shard_map/all_to_all | solution.py:276
  123.5 0.1 reshape.50
  123.6 0.6 fusion.1
  (23 shorter events, 0.2 us)
Async XLA Ops:
  2.0 20.9 %all-to-all-start = ((bf16[32,2,256]{2,1,0:T(2,128)(2,1)}), bf16[32,2,256]{2,1,0:T(2,128)(2,1)S(1)}, u32[]{:S(2)}, u32[]{:S(2)}) async-start(bf16[32,2,256]{2,1,0:T(2,128)(2,1)} %bitcast.1), calls=%async_computation | async-start | bytes 65536 | tf_op jit(solution)/shard_map/all_to_all | solution.py:246
  17.7 38.5 %copy-start = (s32[1,4]{1,0:T(1,128)S(1)}, s32[1,4]{1,0:T(1,128)}, u32[]{:S(2)}) copy-start(s32[1,4]{1,0:T(1,128)} %len_ref.1) | copy-start | bytes 52
  22.9 33.3 %all-to-all-start.1 = ((bf16[8,32,2304]{2,1,0:T(8,128)(2,1)}), bf16[8,32,2304]{2,1,0:T(8,128)(2,1)S(1)}, u32[]{:S(2)}, u32[]{:S(2)}) async-start(bf16[8,32,2304]{2,1,0:T(8,128)(2,1)} %pack.1), calls=%async_computation.1 | async-start | bytes 2359296 | tf_op jit(solution)/shard_map/all_to_all | solution.py:257
  27.1 15.7 %collective-permute-start.2 = (bf16[64,256]{1,0:T(8,128)(2,1)S(1)}, bf16[64,256]{1,0:T(8,128)(2,1)S(1)}, u32[]{:S(2)}, u32[]{:S(2)}) collective-permute-start(bf16[64,256]{1,0:T(8,128)(2,1)S(1)} %reshape.48), channel_id=1, source_target_pairs={{0,384},{128,256},{256,128},{384,0},{1,385},{129,257},{257,129},{3... | collective-permute-start | bytes 98312 | tf_op jit(solution)/shard_map/ppermute | solution.py:197
  32.2 10.6 %collective-permute-start.1 = (bf16[64,256]{1,0:T(8,128)(2,1)S(1)}, bf16[64,256]{1,0:T(8,128)(2,1)S(1)}, u32[]{:S(2)}, u32[]{:S(2)}) collective-permute-start(bf16[64,256]{1,0:T(8,128)(2,1)S(1)} %reshape.48), channel_id=1, source_target_pairs={{0,256},{128,384},{256,0},{384,128},{1,257},{129,385},{257,1},{385... | collective-permute-start | bytes 98312 | tf_op jit(solution)/shard_map/ppermute | solution.py:197
  36.6 6.2 %collective-permute-start = (bf16[64,256]{1,0:T(8,128)(2,1)S(1)}, bf16[64,256]{1,0:T(8,128)(2,1)S(1)}, u32[]{:S(2)}, u32[]{:S(2)}) collective-permute-start(bf16[64,256]{1,0:T(8,128)(2,1)S(1)} %reshape.48), channel_id=1, source_target_pairs={{0,128},{128,0},{256,384},{384,256},{1,129},{129,1},{257,385},{385... | collective-permute-start | bytes 98312 | tf_op jit(solution)/shard_map/ppermute | solution.py:197
  42.8 9.0 %collective-permute-start.5 = (bf16[256,256]{1,0:T(8,128)(2,1)S(1)}, bf16[256,256]{1,0:T(8,128)(2,1)S(1)}, u32[]{:S(2)}, u32[]{:S(2)}) collective-permute-start(bf16[256,256]{1,0:T(8,128)(2,1)S(1)} %constant_dynamic-update-slice_fusion.rest_0_), channel_id=1, source_target_pairs={{0,48},{16,32},{32,16},{48,0},{1,49},{17,33},{33,17},{49,1},{2,50}... | collective-permute-start | bytes 393224 | tf_op jit(solution)/shard_map/ppermute | solution.py:197
  47.2 7.2 %collective-permute-start.4 = (bf16[256,256]{1,0:T(8,128)(2,1)S(1)}, bf16[256,256]{1,0:T(8,128)(2,1)S(1)}, u32[]{:S(2)}, u32[]{:S(2)}) collective-permute-start(bf16[256,256]{1,0:T(8,128)(2,1)S(1)} %constant_dynamic-update-slice_fusion.rest_0_), channel_id=1, source_target_pairs={{0,32},{16,48},{32,0},{48,16},{1,33},{17,49},{33,1},{49,17},{2,34}... | collective-permute-start | bytes 393224 | tf_op jit(solution)/shard_map/ppermute | solution.py:197
  49.7 6.5 %collective-permute-start.3 = (bf16[256,256]{1,0:T(8,128)(2,1)S(1)}, bf16[256,256]{1,0:T(8,128)(2,1)S(1)}, u32[]{:S(2)}, u32[]{:S(2)}) collective-permute-start(bf16[256,256]{1,0:T(8,128)(2,1)S(1)} %constant_dynamic-update-slice_fusion.rest_0_), channel_id=1, source_target_pairs={{0,16},{16,0},{32,48},{48,32},{1,17},{17,1},{33,49},{49,33},{2,18}... | collective-permute-start | bytes 393224 | tf_op jit(solution)/shard_map/ppermute | solution.py:197
  69.0 38.5 %all-to-all-start.2 = ((bf16[8,32,2304]{2,1,0:T(8,128)(2,1)}), bf16[8,32,2304]{2,1,0:T(8,128)(2,1)S(1)}, u32[]{:S(2)}, u32[]{:S(2)}) async-start(bf16[8,32,2304]{2,1,0:T(8,128)(2,1)} %get-tuple-element.25), calls=%async_computation.2 | async-start | bytes 2359296 | tf_op jit(solution)/shard_map/all_to_all | solution.py:265
  76.4 9.6 %collective-permute-start.6 = (bf16[256,256]{1,0:T(8,128)(2,1)S(1)}, bf16[256,256]{1,0:T(8,128)(2,1)S(1)}, u32[]{:S(2)}, u32[]{:S(2)}) collective-permute-start(bf16[256,256]{1,0:T(8,128)(2,1)S(1)} %get-tuple-element.22), channel_id=1, source_target_pairs={{0,16},{16,0},{32,48},{48,32},{1,17},{17,1},{33,49},{49,33},{2,18}... | collective-permute-start | bytes 393224 | tf_op jit(solution)/shard_map/ppermute | solution.py:197
  78.6 9.2 %collective-permute-start.7 = (bf16[256,256]{1,0:T(8,128)(2,1)S(1)}, bf16[256,256]{1,0:T(8,128)(2,1)S(1)}, u32[]{:S(2)}, u32[]{:S(2)}) collective-permute-start(bf16[256,256]{1,0:T(8,128)(2,1)S(1)} %get-tuple-element.23), channel_id=1, source_target_pairs={{0,32},{16,48},{32,0},{48,16},{1,33},{17,49},{33,1},{49,17},{2,34}... | collective-permute-start | bytes 393224 | tf_op jit(solution)/shard_map/ppermute | solution.py:197
  83.2 7.6 %collective-permute-start.8 = (bf16[256,256]{1,0:T(8,128)(2,1)S(1)}, bf16[256,256]{1,0:T(8,128)(2,1)S(1)}, u32[]{:S(2)}, u32[]{:S(2)}) collective-permute-start(bf16[256,256]{1,0:T(8,128)(2,1)S(1)} %get-tuple-element.24), channel_id=1, source_target_pairs={{0,48},{16,32},{32,16},{48,0},{1,49},{17,33},{33,17},{49,1},{2,50}... | collective-permute-start | bytes 393224 | tf_op jit(solution)/shard_map/ppermute | solution.py:197
  90.9 11.4 %collective-permute-start.9 = (bf16[64,256]{1,0:T(8,128)(2,1)S(1)}, bf16[64,256]{1,0:T(8,128)(2,1)S(1)}, u32[]{:S(2)}, u32[]{:S(2)}) collective-permute-start(bf16[64,256]{1,0:T(8,128)(2,1)S(1)} %get-tuple-element.32), channel_id=1, source_target_pairs={{0,128},{128,0},{256,384},{384,256},{1,129},{129,1},{257,385},{385... | collective-permute-start | bytes 98312 | tf_op jit(solution)/shard_map/ppermute | solution.py:197
  92.9 9.4 %collective-permute-start.11 = (bf16[64,256]{1,0:T(8,128)(2,1)S(1)}, bf16[64,256]{1,0:T(8,128)(2,1)S(1)}, u32[]{:S(2)}, u32[]{:S(2)}) collective-permute-start(bf16[64,256]{1,0:T(8,128)(2,1)S(1)} %get-tuple-element.33), channel_id=1, source_target_pairs={{0,384},{128,256},{256,128},{384,0},{1,385},{129,257},{257,129},{3... | collective-permute-start | bytes 98312 | tf_op jit(solution)/shard_map/ppermute | solution.py:197
  97.9 8.9 %collective-permute-start.10 = (bf16[64,256]{1,0:T(8,128)(2,1)S(1)}, bf16[64,256]{1,0:T(8,128)(2,1)S(1)}, u32[]{:S(2)}, u32[]{:S(2)}) collective-permute-start(bf16[64,256]{1,0:T(8,128)(2,1)S(1)} %get-tuple-element.34), channel_id=1, source_target_pairs={{0,256},{128,384},{256,0},{384,128},{1,257},{129,385},{257,1},{385... | collective-permute-start | bytes 98312 | tf_op jit(solution)/shard_map/ppermute | solution.py:197
  107.5 8.0 %copy-start.1 = (bf16[8,32,2304]{2,1,0:T(8,128)(2,1)}, bf16[8,32,2304]{2,1,0:T(8,128)(2,1)S(1)}, u32[]{:S(2)}) copy-start(bf16[8,32,2304]{2,1,0:T(8,128)(2,1)S(1)} %all-to-all-done.2.blocks) | copy-start | bytes 3538948
  107.5 16.0 %all-to-all-start.3 = ((f32[32,2,256]{2,1,0:T(2,128)}), f32[32,2,256]{2,1,0:T(2,128)S(1)}, u32[]{:S(2)}, u32[]{:S(2)}) async-start(f32[32,2,256]{2,1,0:T(2,128)} %reshape.49), calls=%async_computation.3 | async-start | bytes 131072 | tf_op jit(solution)/shard_map/all_to_all | solution.py:276

commit v4 on v3

--- a/solution.py
+++ b/solution.py
@@ -9,8 +9,10 @@
 from jax.sharding import Mesh, PartitionSpec as P
 
 DH = 128
-AXES = ("y_lo", "y_hi", "x", "z_hi", "z_lo", "core")
-FIRST_AXES = ("y_hi", "z_hi", "z_lo", "core")
+AXES = ("y4", "y2", "y1", "x", "z_hi", "z_lo", "core")
+RESP_AXES = ("y4", "y2", "y1", "x", "z_hi")
+FIRST_AXES = ("y1", "z_hi", "z_lo", "core")
+LAST_AXES = ("y2",) + FIRST_AXES
 HEAD_AXES = ("z_lo", "core")
 PEERS = 8
 SLOTS = 4
@@ -20,6 +22,7 @@
 BLOCK_COLS = 2 * QCOLS + 2 * DH
 OWN = PEERS * ROWS
 FIRST = 32
+LAST = 64
 XS = 4
 XROWS = 256
 PROMPT = XS * XROWS
@@ -257,7 +260,8 @@
     held = lax.all_to_all(packed, HEAD_AXES, split_axis=0, concat_axis=0, tiled=True)
 
     line = line.reshape(FIRST * own_rows, 2 * DH)
-    line = jnp.concatenate([line] + [across(line, "y_lo", b) for b in (1, 2, 3)], axis=0)
+    for axis in ("y4", "y2"):
+        line = jnp.concatenate([line, across(line, axis, 1)], axis=0)
     prompt = [line] + [across(line, "x", a) for a in (1, 2, 3)]
 
     made, *parts = attend(lengths, held, prompt)
@@ -267,14 +271,12 @@
     total = parts[0].astype(f32)
     for a in (1, 2, 3):
         total = total + across(parts[a], "x", a).astype(f32)
-    total = total.astype(bf16).reshape(4, XROWS // 4, 2 * DH)
-    pieces = [total[b] for b in range(4)]
-    total = pieces[0].astype(f32)
-    for b in (1, 2, 3):
-        total = total + across(pieces[b], "y_lo", b).astype(f32)
-    total, back = lax.optimization_barrier((total.reshape(FIRST, own_rows, 2 * DH), back))
-    owned = lax.all_to_all(total, FIRST_AXES, split_axis=0, concat_axis=0, tiled=True)
-    owned = jnp.sum(owned.reshape(4, PEERS, own_rows, 2, DH), axis=0)
+    total = total.astype(bf16).reshape(2, 2, XROWS // 4, 2 * DH)
+    total = total[:, 0].astype(f32) + across(total[:, 1], "y4", 1).astype(f32)
+    total = jnp.where(lax.axis_index("y2") == 0, total, total[::-1])
+    total, back = lax.optimization_barrier((total.reshape(LAST, own_rows, 2 * DH), back))
+    owned = lax.all_to_all(total, LAST_AXES, split_axis=0, concat_axis=0, tiled=True)
+    owned = jnp.sum(owned.reshape(LAST // PEERS, PEERS, own_rows, 2, DH), axis=0)
     owned = owned.transpose(2, 1, 0, 3).reshape(2, own_rows, PEERS * DH)
 
     results = pl.pallas_call(
@@ -289,12 +291,12 @@
 
 
 def solution(mesh):
-    fine = Mesh(mesh.devices.reshape(4, 2, 4, 2, 4, 2), AXES)
+    fine = Mesh(mesh.devices.reshape(2, 2, 2, 4, 2, 4, 2), AXES)
     rows = P(AXES, None)
     return jax.shard_map(
         on_device,
         mesh=fine,
-        in_specs=(rows,) * 6 + (P(("y_lo", "y_hi", "x", "z_hi"), None),),
+        in_specs=(rows,) * 6 + (P(RESP_AXES, None),),
         out_specs=(rows,) * 6,
         check_vma=False,
     )

time: 125 us -> 124 us (level)
  starting transfers between devices: 74 us -> 69.1 us
  waiting for transfers between devices: 28.3 us -> 32.6 us
    all_to_all x1, waiting for transfers between devices: 0.01 us -> 5.88 us  [on_device(): lax.all_to_all(made, HEAD_AXES, split_axis=0, concat_axis=0, tiled=True)]
    ppermute x12 -> x9, starting transfers between devices: 41.3 us -> 37.7 us  [across(): return lax.ppermute(value, axis, [(i, i ^ s) for i in range(n)])]
    ppermute x12 -> x9, waiting for transfers between devices: 17.8 us -> 14.2 us  [across(): return lax.ppermute(value, axis, [(i, i ^ s) for i in range(n)])]
    all_to_all x1, starting transfers between devices: 8.03 us -> 5.66 us  [on_device(): lax.all_to_all(total, LAST_AXES, split_axis=0, concat_axis=0, tiled=True)]
    all_to_all x1, waiting for transfers between devices: 5.28 us -> 7.33 us  [on_device(): lax.all_to_all(total, LAST_AXES, split_axis=0, concat_axis=0, tiled=True)]
  transfers between devices with their start and end apart: 16 -> 13, of which waited for: 8 -> 10; matrix products, arithmetic and copies ran while one was open for 1% -> 1% of each run, Pallas kernels for 4% -> 4%
where the time goes in v4:
time: 124 us
  starting transfers between devices  69.1 us (56%)
  waiting for transfers between devices  32.6 us (26%)
  Pallas kernels  18.1 us (15%)
  local copies, waits for them, and re-layouts  2.88 us (2%)
    ppermute x9, starting transfers between devices, across(): return lax.ppermute(value, axis, [(i, i ^ s) for i in range(n)])  37.7 us
    ppermute x9, waiting for transfers between devices, across(): return lax.ppermute(value, axis, [(i, i ^ s) for i in range(n)])  14.2 us
    all_to_all x1, starting transfers between devices, on_device(): lax.all_to_all(by_head, FIRST_AXES, split_axis=0, concat_axis=0, tiled=True)  13 us
    pallas_call x1, Pallas kernels, attend(): pl.pallas_call(attend_kernel, out_shape=[block] + [piece] * XS, in_specs=...  12.8 us
    all_to_all x1, starting transfers between devices, on_device(): lax.all_to_all(made, HEAD_AXES, split_axis=0, concat_axis=0, tiled=True)  8.58 us
    all_to_all x1, waiting for transfers between devices, on_device(): lax.all_to_all(total, LAST_AXES, split_axis=0, concat_axis=0, tiled=True)  7.33 us
    all_to_all x1, waiting for transfers between devices, on_device(): lax.all_to_all(made, HEAD_AXES, split_axis=0, concat_axis=0, tiled=True)  5.88 us
    all_to_all x1, starting transfers between devices, on_device(): lax.all_to_all(total, LAST_AXES, split_axis=0, concat_axis=0, tiled=True)  5.66 us
  transfers between devices with their start and end apart: 13, of which 10 were waited for; matrix products, arithmetic and copies ran while one was open for 1% of the time, Pallas kernels for 4%

profile of v4, /device:TPU:1, one launch (start us, length us, event | category | flops | bytes accessed | tf_op | source)
XLA Modules:
  0.0 123.7 jit_solution(2747260004013020585)
XLA Ops:
  0.6 0.7 copy_bitcast_fusion
  1.4 0.6 broadcast_in_dim.2
  2.0 13.0 %all-to-all-start = ((bf16[32,2,256]{2,1,0:T(2,128)(2,1)}), bf16[32,2,256]{2,1,0:T(2,128)(2,1)S(1)}, u32[]{:S(2)}, u32[]{:S(2)}) async-start(bf16[32,2,256]{2,1,0:T(2,128)(2,1)} %bitcast.1), calls=%async_computation | async-start | bytes 65536 | tf_op jit(solution)/shard_map/all_to_all | solution.py:249
  15.0 2.7 %pack.1 = bf16[8,32,2304]{2,1,0:T(8,128)(2,1)} custom-call(bf16[32,8192]{1,0:T(8,128)(2,1)} %q_ref.1, bf16[32,8192]{1,0:T(8,128)(2,1)} %g_ref.1, bf16[32,1024]{1,0:T(8,128)(2,1)} %k_ref.1, bf16[32,1024]{1,0:T(8,128)(2,1)} %v_ref.1), custom_call_target="tpu_custom_call" | custom-call | tf_op jit(solution)/shard_map/pack/pallas_call | solution.py:251
  17.7 5.2 %all-to-all-done = bf16[32,2,256]{2,1,0:T(2,128)(2,1)S(1)} async-done(((bf16[32,2,256]{2,1,0:T(2,128)(2,1)}), bf16[32,2,256]{2,1,0:T(2,128)(2,1)S(1)}, u32[]{:S(2)}, u32[]{:S(2)}) %all-to-all-start) | async-done | bytes 32800 | tf_op jit(solution)/shard_map/all_to_all | solution.py:249
  22.9 4.3 %all-to-all-start.1 = ((bf16[8,32,2304]{2,1,0:T(8,128)(2,1)}), bf16[8,32,2304]{2,1,0:T(8,128)(2,1)S(1)}, u32[]{:S(2)}, u32[]{:S(2)}) async-start(bf16[8,32,2304]{2,1,0:T(8,128)(2,1)} %pack.1), calls=%async_computation.1 | async-start | bytes 2359296 | tf_op jit(solution)/shard_map/all_to_all | solution.py:260
  27.1 6.6 %collective-permute-start = (bf16[64,256]{1,0:T(8,128)(2,1)S(1)}, bf16[64,256]{1,0:T(8,128)(2,1)S(1)}, u32[]{:S(2)}, u32[]{:S(2)}) collective-permute-start(bf16[64,256]{1,0:T(8,128)(2,1)S(1)} %reshape.44), channel_id=1, source_target_pairs={{0,256},{256,0},{1,257},{257,1},{2,258},{258,2},{3,259},{259,3},{4... | collective-permute-start | bytes 98312 | tf_op jit(solution)/shard_map/ppermute | solution.py:200
  33.7 2.0 %collective-permute-done = bf16[64,256]{1,0:T(8,128)(2,1)S(1)} collective-permute-done((bf16[64,256]{1,0:T(8,128)(2,1)S(1)}, bf16[64,256]{1,0:T(8,128)(2,1)S(1)}, u32[]{:S(2)}, u32[]{:S(2)}) %collective-permute-start) | collective-permute-done | bytes 32800 | tf_op jit(solution)/shard_map/ppermute | solution.py:200
  35.8 5.1 %collective-permute-start.1 = (bf16[128,256]{1,0:T(8,128)(2,1)S(1)}, bf16[128,256]{1,0:T(8,128)(2,1)S(1)}, u32[]{:S(2)}, u32[]{:S(2)}) collective-permute-start(bf16[128,256]{1,0:T(8,128)(2,1)S(1)} %pad_maximum_fusion), channel_id=1, source_target_pairs={{0,128},{128,0},{1,129},{129,1},{2,130},{130,2},{3,131},{131,3},{4... | collective-permute-start | bytes 196616 | tf_op jit(solution)/shard_map/ppermute | solution.py:200
  40.9 1.9 %collective-permute-done.1 = bf16[128,256]{1,0:T(8,128)(2,1)S(1)} collective-permute-done((bf16[128,256]{1,0:T(8,128)(2,1)S(1)}, bf16[128,256]{1,0:T(8,128)(2,1)S(1)}, u32[]{:S(2)}, u32[]{:S(2)}) %collective-permute-start.1) | collective-permute-done | bytes 65568 | tf_op jit(solution)/shard_map/ppermute | solution.py:200
  42.8 3.1 %collective-permute-start.2 = (bf16[256,256]{1,0:T(8,128)(2,1)S(1)}, bf16[256,256]{1,0:T(8,128)(2,1)S(1)}, u32[]{:S(2)}, u32[]{:S(2)}) collective-permute-start(bf16[256,256]{1,0:T(8,128)(2,1)S(1)} %constant_dynamic-update-slice_fusion.rest_0_), channel_id=1, source_target_pairs={{0,16},{16,0},{32,48},{48,32},{1,17},{17,1},{33,49},{49,33},{2,18}... | collective-permute-start | bytes 393224 | tf_op jit(solution)/shard_map/ppermute | solution.py:200
  45.9 4.4 %collective-permute-start.3 = (bf16[256,256]{1,0:T(8,128)(2,1)S(1)}, bf16[256,256]{1,0:T(8,128)(2,1)S(1)}, u32[]{:S(2)}, u32[]{:S(2)}) collective-permute-start(bf16[256,256]{1,0:T(8,128)(2,1)S(1)} %constant_dynamic-update-slice_fusion.rest_0_), channel_id=1, source_target_pairs={{0,32},{16,48},{32,0},{48,16},{1,33},{17,49},{33,1},{49,17},{2,34}... | collective-permute-start | bytes 393224 | tf_op jit(solution)/shard_map/ppermute | solution.py:200
  50.3 2.1 %collective-permute-start.4 = (bf16[256,256]{1,0:T(8,128)(2,1)S(1)}, bf16[256,256]{1,0:T(8,128)(2,1)S(1)}, u32[]{:S(2)}, u32[]{:S(2)}) collective-permute-start(bf16[256,256]{1,0:T(8,128)(2,1)S(1)} %constant_dynamic-update-slice_fusion.rest_0_), channel_id=1, source_target_pairs={{0,48},{16,32},{32,16},{48,0},{1,49},{17,33},{33,17},{49,1},{2,50}... | collective-permute-start | bytes 393224 | tf_op jit(solution)/shard_map/ppermute | solution.py:200
  52.4 2.4 %collective-permute-done.3.rest_2_ = bf16[256,256]{1,0:T(8,128)(2,1)S(1)} collective-permute-done((bf16[256,256]{1,0:T(8,128)(2,1)S(1)}, bf16[256,256]{1,0:T(8,128)(2,1)S(1)}, u32[]{:S(2)}, u32[]{:S(2)}) %collective-permute-start.3) | collective-permute-done | bytes 131104 | tf_op jit(solution)/shard_map/ppermute | solution.py:200
  54.9 2.4 %collective-permute-done.4.rest_3_ = bf16[256,256]{1,0:T(8,128)(2,1)S(1)} collective-permute-done((bf16[256,256]{1,0:T(8,128)(2,1)S(1)}, bf16[256,256]{1,0:T(8,128)(2,1)S(1)}, u32[]{:S(2)}, u32[]{:S(2)}) %collective-permute-start.4) | collective-permute-done | bytes 131104 | tf_op jit(solution)/shard_map/ppermute | solution.py:200
  57.3 12.8 %attend.1 = (bf16[8,32,2304]{2,1,0:T(8,128)(2,1)}, bf16[256,256]{1,0:T(8,128)(2,1)S(1)}, bf16[256,256]{1,0:T(8,128)(2,1)S(1)}, bf16[256,256]{1,0:T(8,128)(2,1)S(1)}, bf16[256,256]{1,0:T(8,128)(2,1)S(1)}) custom-call(s32[1,4]{1,0:T(1,128)S(1)} %copy-done, bf16[8,32,2304]{2,1,0:T(8,128)(2,1)S(1)} %all-to-all-done.1.blocks, ...), custom_call_target="tpu_custom_call" | custom-call | flops 4026531840 | bytes 4194304 | tf_op jit(solution)/shard_map/attend/pallas_call | solution.py:207
  70.1 8.6 %all-to-all-start.2 = ((bf16[8,32,2304]{2,1,0:T(8,128)(2,1)}), bf16[8,32,2304]{2,1,0:T(8,128)(2,1)S(1)}, u32[]{:S(2)}, u32[]{:S(2)}) async-start(bf16[8,32,2304]{2,1,0:T(8,128)(2,1)} %get-tuple-element.25), calls=%async_computation.2 | async-start | bytes 2359296 | tf_op jit(solution)/shard_map/all_to_all | solution.py:269
  78.7 1.9 %collective-permute-start.5 = (bf16[256,256]{1,0:T(8,128)(2,1)S(1)}, bf16[256,256]{1,0:T(8,128)(2,1)S(1)}, u32[]{:S(2)}, u32[]{:S(2)}) collective-permute-start(bf16[256,256]{1,0:T(8,128)(2,1)S(1)} %get-tuple-element.22), channel_id=1, source_target_pairs={{0,16},{16,0},{32,48},{48,32},{1,17},{17,1},{33,49},{49,33},{2,18}... | collective-permute-start | bytes 393224 | tf_op jit(solution)/shard_map/ppermute | solution.py:200
  80.6 3.3 %collective-permute-start.6 = (bf16[256,256]{1,0:T(8,128)(2,1)S(1)}, bf16[256,256]{1,0:T(8,128)(2,1)S(1)}, u32[]{:S(2)}, u32[]{:S(2)}) collective-permute-start(bf16[256,256]{1,0:T(8,128)(2,1)S(1)} %get-tuple-element.23), channel_id=1, source_target_pairs={{0,32},{16,48},{32,0},{48,16},{1,33},{17,49},{33,1},{49,17},{2,34}... | collective-permute-start | bytes 393224 | tf_op jit(solution)/shard_map/ppermute | solution.py:200
  83.9 4.4 %collective-permute-start.7 = (bf16[256,256]{1,0:T(8,128)(2,1)S(1)}, bf16[256,256]{1,0:T(8,128)(2,1)S(1)}, u32[]{:S(2)}, u32[]{:S(2)}) collective-permute-start(bf16[256,256]{1,0:T(8,128)(2,1)S(1)} %get-tuple-element.24), channel_id=1, source_target_pairs={{0,48},{16,32},{32,16},{48,0},{1,49},{17,33},{33,17},{49,1},{2,50}... | collective-permute-start | bytes 393224 | tf_op jit(solution)/shard_map/ppermute | solution.py:200
  88.3 0.8 collective-permute-done.6
  89.1 2.4 %collective-permute-done.7 = bf16[256,256]{1,0:T(8,128)(2,1)S(1)} collective-permute-done((bf16[256,256]{1,0:T(8,128)(2,1)S(1)}, bf16[256,256]{1,0:T(8,128)(2,1)S(1)}, u32[]{:S(2)}, u32[]{:S(2)}) %collective-permute-start.7) | collective-permute-done | bytes 131104 | tf_op jit(solution)/shard_map/ppermute | solution.py:200
  91.5 0.1 add_convert_fusion
  91.6 6.8 %collective-permute-start.8 = (bf16[2,64,256]{2,1,0:T(8,128)(2,1)S(1)}, bf16[2,64,256]{2,1,0:T(8,128)(2,1)S(1)}, u32[]{:S(2)}, u32[]{:S(2)}) collective-permute-start(bf16[2,64,256]{2,1,0:T(8,128)(2,1)S(1)} %slice_bitcast_fusion), channel_id=1, source_target_pairs={{0,256},{256,0},{1,257},{257,1},{2,258},{258,2},{3,259},{259,3},{4... | collective-permute-start | bytes 196616 | tf_op jit(solution)/shard_map/ppermute | solution.py:200
  98.4 2.2 %collective-permute-done.8 = bf16[2,64,256]{2,1,0:T(8,128)(2,1)S(1)} collective-permute-done((bf16[2,64,256]{2,1,0:T(8,128)(2,1)S(1)}, bf16[2,64,256]{2,1,0:T(8,128)(2,1)S(1)}, u32[]{:S(2)}, u32[]{:S(2)}) %collective-permute-start.8) | collective-permute-done | bytes 65568 | tf_op jit(solution)/shard_map/ppermute | solution.py:200
  100.6 0.7 reshape.46
  101.4 5.9 %all-to-all-done.2.blocks = bf16[8,32,2304]{2,1,0:T(8,128)(2,1)S(1)} async-done(((bf16[8,32,2304]{2,1,0:T(8,128)(2,1)}), bf16[8,32,2304]{2,1,0:T(8,128)(2,1)S(1)}, u32[]{:S(2)}, u32[]{:S(2)}) %all-to-all-start.2) | async-done | bytes 1179680 | tf_op jit(solution)/shard_map/all_to_all | solution.py:269
  107.2 5.7 %all-to-all-start.3 = ((f32[64,2,256]{2,1,0:T(2,128)}), f32[64,2,256]{2,1,0:T(2,128)S(1)}, u32[]{:S(2)}, u32[]{:S(2)}) async-start(f32[64,2,256]{2,1,0:T(2,128)} %reshape.46), calls=%async_computation.3 | async-start | bytes 262144 | tf_op jit(solution)/shard_map/all_to_all | solution.py:278
  112.9 2.6 %unpack.1 = (bf16[32,8192]{1,0:T(8,128)(2,1)}, bf16[32,8192]{1,0:T(8,128)(2,1)}, bf16[32,1024]{1,0:T(8,128)(2,1)}, bf16[32,1024]{1,0:T(8,128)(2,1)}) custom-call(bf16[8,32,2304]{2,1,0:T(8,128)(2,1)} %copy-done.1), custom_call_target="tpu_custom_call" | custom-call | tf_op jit(solution)/shard_map/unpack/pallas_call | solution.py:282
  115.6 7.3 %all-to-all-done.3 = f32[64,2,256]{2,1,0:T(2,128)S(1)} async-done(((f32[64,2,256]{2,1,0:T(2,128)}), f32[64,2,256]{2,1,0:T(2,128)S(1)}, u32[]{:S(2)}, u32[]{:S(2)}) %all-to-all-start.3) | async-done | bytes 131104 | tf_op jit(solution)/shard_map/all_to_all | solution.py:278
  122.9 0.2 reshape.47
  123.1 0.6 fusion
  (18 shorter events, 0.2 us)
Async XLA Ops:
  2.0 20.9 %all-to-all-start = ((bf16[32,2,256]{2,1,0:T(2,128)(2,1)}), bf16[32,2,256]{2,1,0:T(2,128)(2,1)S(1)}, u32[]{:S(2)}, u32[]{:S(2)}) async-start(bf16[32,2,256]{2,1,0:T(2,128)(2,1)} %bitcast.1), calls=%async_computation | async-start | bytes 65536 | tf_op jit(solution)/shard_map/all_to_all | solution.py:249
  17.7 39.6 %copy-start = (s32[1,4]{1,0:T(1,128)S(1)}, s32[1,4]{1,0:T(1,128)}, u32[]{:S(2)}) copy-start(s32[1,4]{1,0:T(1,128)} %len_ref.1) | copy-start | bytes 52
  22.9 34.4 %all-to-all-start.1 = ((bf16[8,32,2304]{2,1,0:T(8,128)(2,1)}), bf16[8,32,2304]{2,1,0:T(8,128)(2,1)S(1)}, u32[]{:S(2)}, u32[]{:S(2)}) async-start(bf16[8,32,2304]{2,1,0:T(8,128)(2,1)} %pack.1), calls=%async_computation.1 | async-start | bytes 2359296 | tf_op jit(solution)/shard_map/all_to_all | solution.py:260
  27.1 8.6 %collective-permute-start = (bf16[64,256]{1,0:T(8,128)(2,1)S(1)}, bf16[64,256]{1,0:T(8,128)(2,1)S(1)}, u32[]{:S(2)}, u32[]{:S(2)}) collective-permute-start(bf16[64,256]{1,0:T(8,128)(2,1)S(1)} %reshape.44), channel_id=1, source_target_pairs={{0,256},{256,0},{1,257},{257,1},{2,258},{258,2},{3,259},{259,3},{4... | collective-permute-start | bytes 98312 | tf_op jit(solution)/shard_map/ppermute | solution.py:200
  35.8 7.1 %collective-permute-start.1 = (bf16[128,256]{1,0:T(8,128)(2,1)S(1)}, bf16[128,256]{1,0:T(8,128)(2,1)S(1)}, u32[]{:S(2)}, u32[]{:S(2)}) collective-permute-start(bf16[128,256]{1,0:T(8,128)(2,1)S(1)} %pad_maximum_fusion), channel_id=1, source_target_pairs={{0,128},{128,0},{1,129},{129,1},{2,130},{130,2},{3,131},{131,3},{4... | collective-permute-start | bytes 196616 | tf_op jit(solution)/shard_map/ppermute | solution.py:200
  42.8 9.6 %collective-permute-start.2 = (bf16[256,256]{1,0:T(8,128)(2,1)S(1)}, bf16[256,256]{1,0:T(8,128)(2,1)S(1)}, u32[]{:S(2)}, u32[]{:S(2)}) collective-permute-start(bf16[256,256]{1,0:T(8,128)(2,1)S(1)} %constant_dynamic-update-slice_fusion.rest_0_), channel_id=1, source_target_pairs={{0,16},{16,0},{32,48},{48,32},{1,17},{17,1},{33,49},{49,33},{2,18}... | collective-permute-start | bytes 393224 | tf_op jit(solution)/shard_map/ppermute | solution.py:200
  45.9 8.9 %collective-permute-start.3 = (bf16[256,256]{1,0:T(8,128)(2,1)S(1)}, bf16[256,256]{1,0:T(8,128)(2,1)S(1)}, u32[]{:S(2)}, u32[]{:S(2)}) collective-permute-start(bf16[256,256]{1,0:T(8,128)(2,1)S(1)} %constant_dynamic-update-slice_fusion.rest_0_), channel_id=1, source_target_pairs={{0,32},{16,48},{32,0},{48,16},{1,33},{17,49},{33,1},{49,17},{2,34}... | collective-permute-start | bytes 393224 | tf_op jit(solution)/shard_map/ppermute | solution.py:200
  50.3 7.0 %collective-permute-start.4 = (bf16[256,256]{1,0:T(8,128)(2,1)S(1)}, bf16[256,256]{1,0:T(8,128)(2,1)S(1)}, u32[]{:S(2)}, u32[]{:S(2)}) collective-permute-start(bf16[256,256]{1,0:T(8,128)(2,1)S(1)} %constant_dynamic-update-slice_fusion.rest_0_), channel_id=1, source_target_pairs={{0,48},{16,32},{32,16},{48,0},{1,49},{17,33},{33,17},{49,1},{2,50}... | collective-permute-start | bytes 393224 | tf_op jit(solution)/shard_map/ppermute | solution.py:200
  70.1 37.1 %all-to-all-start.2 = ((bf16[8,32,2304]{2,1,0:T(8,128)(2,1)}), bf16[8,32,2304]{2,1,0:T(8,128)(2,1)S(1)}, u32[]{:S(2)}, u32[]{:S(2)}) async-start(bf16[8,32,2304]{2,1,0:T(8,128)(2,1)} %get-tuple-element.25), calls=%async_computation.2 | async-start | bytes 2359296 | tf_op jit(solution)/shard_map/all_to_all | solution.py:269
  78.7 9.6 %collective-permute-start.5 = (bf16[256,256]{1,0:T(8,128)(2,1)S(1)}, bf16[256,256]{1,0:T(8,128)(2,1)S(1)}, u32[]{:S(2)}, u32[]{:S(2)}) collective-permute-start(bf16[256,256]{1,0:T(8,128)(2,1)S(1)} %get-tuple-element.22), channel_id=1, source_target_pairs={{0,16},{16,0},{32,48},{48,32},{1,17},{17,1},{33,49},{49,33},{2,18}... | collective-permute-start | bytes 393224 | tf_op jit(solution)/shard_map/ppermute | solution.py:200
  80.6 8.5 %collective-permute-start.6 = (bf16[256,256]{1,0:T(8,128)(2,1)S(1)}, bf16[256,256]{1,0:T(8,128)(2,1)S(1)}, u32[]{:S(2)}, u32[]{:S(2)}) collective-permute-start(bf16[256,256]{1,0:T(8,128)(2,1)S(1)} %get-tuple-element.23), channel_id=1, source_target_pairs={{0,32},{16,48},{32,0},{48,16},{1,33},{17,49},{33,1},{49,17},{2,34}... | collective-permute-start | bytes 393224 | tf_op jit(solution)/shard_map/ppermute | solution.py:200
  83.9 7.6 %collective-permute-start.7 = (bf16[256,256]{1,0:T(8,128)(2,1)S(1)}, bf16[256,256]{1,0:T(8,128)(2,1)S(1)}, u32[]{:S(2)}, u32[]{:S(2)}) collective-permute-start(bf16[256,256]{1,0:T(8,128)(2,1)S(1)} %get-tuple-element.24), channel_id=1, source_target_pairs={{0,48},{16,32},{32,16},{48,0},{1,49},{17,33},{33,17},{49,1},{2,50}... | collective-permute-start | bytes 393224 | tf_op jit(solution)/shard_map/ppermute | solution.py:200
  91.6 9.0 %collective-permute-start.8 = (bf16[2,64,256]{2,1,0:T(8,128)(2,1)S(1)}, bf16[2,64,256]{2,1,0:T(8,128)(2,1)S(1)}, u32[]{:S(2)}, u32[]{:S(2)}) collective-permute-start(bf16[2,64,256]{2,1,0:T(8,128)(2,1)S(1)} %slice_bitcast_fusion), channel_id=1, source_target_pairs={{0,256},{256,0},{1,257},{257,1},{2,258},{258,2},{3,259},{259,3},{4... | collective-permute-start | bytes 196616 | tf_op jit(solution)/shard_map/ppermute | solution.py:200
  107.2 5.7 %copy-start.1 = (bf16[8,32,2304]{2,1,0:T(8,128)(2,1)}, bf16[8,32,2304]{2,1,0:T(8,128)(2,1)S(1)}, u32[]{:S(2)}) copy-start(bf16[8,32,2304]{2,1,0:T(8,128)(2,1)S(1)} %all-to-all-done.2.blocks) | copy-start | bytes 3538948
  107.2 15.7 %all-to-all-start.3 = ((f32[64,2,256]{2,1,0:T(2,128)}), f32[64,2,256]{2,1,0:T(2,128)S(1)}, u32[]{:S(2)}, u32[]{:S(2)}) async-start(f32[64,2,256]{2,1,0:T(2,128)} %reshape.46), calls=%async_computation.3 | async-start | bytes 262144 | tf_op jit(solution)/shard_map/all_to_all | solution.py:278
